TPU v7x, 32 devices: a whole 2x2x4 slice. The times are simulated.
32 devices in a mesh: gx: 8 (over z, core), gy: 4 (over y, x).
Axes of the slice: x: 2, y: 2, z: 4, core: 2. Of those that a mesh axis runs over, the one named last changes fastest.
Arguments:
- field: bfloat16 [64, 32, 16, 256], P(None, 'gx', 'gy'), may hold values from -6 to 6
- weight_first: bfloat16 [64, 1728], replicated, may hold values from -0.15625 to 0.15625
- weight_down: bfloat16 [128, 512], replicated, may hold values from -0.25 to 0.25
- weight_coarse: bfloat16 [128, 3456], replicated, may hold values from -0.109375 to 0.109375
- weight_up: bfloat16 [64, 1024], replicated, may hold values from -0.5 to 0.5
- weight_last: bfloat16 [64, 1728], replicated, may hold values from -0.15625 to 0.15625
- cotangent: bfloat16 [64, 32, 16, 256], P(None, 'gx', 'gy'), may hold values from -0.016479492 to 0.016479492
Outputs:
- output: bfloat16 [64, 32, 16, 256], P(None, 'gx', 'gy')
- grad_first: float32 [64, 1728], replicated
- grad_down: float32 [128, 512], replicated
- grad_coarse: float32 [128, 3456], replicated
- grad_up: float32 [64, 1024], replicated
- grad_last: float32 [64, 1728], replicated
All inputs are finite; a program needn't handle non-finite values.
Results may differ from a plain program's by a relative error of at most 0.0069.
Values may be sent and summed in bfloat16 or wider, within the bound.
A program may use at most 128 MiB of HBM per device.

v0:
```python
import functools

import jax
import jax.numpy as jnp
from jax import lax
from jax.experimental import pallas as pl
from jax.experimental.pallas import tpu as pltpu
from jax.sharding import PartitionSpec as P

MESH = pl.DeviceIdType.MESH
BF16 = jnp.bfloat16
F32 = jnp.float32
VMEM_BYTES = 56 * 1024 * 1024
LANES = 128


def leaky(values):
    return 0.505 * values + 0.495 * (jnp.sqrt(values * values + 1.0) - 1.0)


def slope_of(values):
    values = values.astype(F32)
    return 0.505 + 0.495 * values * lax.rsqrt(values * values + 1.0)


def dot(left, right):
    return jnp.dot(left, right, preferred_element_type=F32)


def dot_nt(left, right):
    return lax.dot_general(left, right, (((1,), (1,)), ((), ())), preferred_element_type=F32)


def call(kernel, args, outs, scratch, name, collective=None):
    params = dict(vmem_limit_bytes=VMEM_BYTES)
    if collective is not None:
        params.update(collective_id=collective, has_side_effects=True)
    return pl.pallas_call(
        kernel,
        out_shape=outs,
        in_specs=[pl.BlockSpec(memory_space=pltpu.VMEM)] * len(args),
        out_specs=[pl.BlockSpec(memory_space=pltpu.VMEM)] * len(outs),
        scratch_shapes=scratch,
        compiler_params=pltpu.CompilerParams(**params),
        name=name,
    )(*args)


def halo_kernel(sizes, counts, *refs):
    number = len(sizes)
    ins, outs, (send, recv) = refs[:number], refs[number : 2 * number], refs[2 * number :]
    n_x, n_y = counts
    me_x, me_y = lax.axis_index("gx"), lax.axis_index("gy")
    steps = [(i, j) for i in (-1, 0, 1) for j in (-1, 0, 1) if (i, j) != (0, 0)]

    def inside(step_x, step_y):
        at_x, at_y = me_x + step_x, me_y + step_y
        return (at_x >= 0) & (at_x < n_x) & (at_y >= 0) & (at_y < n_y)

    def place(step_x, step_y):
        return (
            jnp.clip(me_x + step_x, 0, n_x - 1),
            jnp.clip(me_y + step_y, 0, n_y - 1),
        )

    barrier = pltpu.get_barrier_semaphore()
    for step in steps:

        @pl.when(inside(*step))
        def _(step=step):
            pl.semaphore_signal(barrier, inc=1, device_id=place(*step), device_id_type=MESH)

    pl.semaphore_wait(barrier, sum(inside(*step).astype(jnp.int32) for step in steps))

    def spans(step, extent, width):
        if step == 0:
            return pl.ds(0, extent), pl.ds(width, extent)
        if step > 0:
            return pl.ds(extent - width, width), pl.ds(0, width)
        return pl.ds(0, width), pl.ds(width + extent, width)

    copies = []
    for at, (step_x, step_y) in enumerate(steps):
        for which, (row_width, lane_width) in enumerate(sizes):
            rows, lanes = ins[which].shape
            row_from, row_to = spans(step_y, rows, row_width)
            lane_from, lane_to = spans(step_x, lanes, lane_width)
            copies.append(
                (
                    step_x,
                    step_y,
                    pltpu.make_async_remote_copy(
                        src_ref=ins[which].at[row_from, lane_from],
                        dst_ref=outs[which].at[row_to, lane_to],
                        send_sem=send.at[at, which],
                        recv_sem=recv.at[at, which],
                        device_id=place(step_x, step_y),
                        device_id_type=MESH,
                    ),
                )
            )
    for step_x, step_y, copy in copies:

        @pl.when(inside(step_x, step_y))
        def _(copy=copy):
            copy.start()

    for which, (row_width, lane_width) in enumerate(sizes):
        rows, lanes = ins[which].shape
        outs[which][row_width : row_width + rows, lane_width : lane_width + lanes] = ins[which][...]
        for step_x, step_y in steps:
            row_at = {-1: (0, row_width), 0: (row_width, rows), 1: (row_width + rows, row_width)}[step_y]
            lane_at = {-1: (0, lane_width), 0: (lane_width, lanes), 1: (lane_width + lanes, lane_width)}[step_x]

            @pl.when(jnp.logical_not(inside(step_x, step_y)))
            def _(row_at=row_at, lane_at=lane_at, which=which):
                outs[which][
                    row_at[0] : row_at[0] + row_at[1], lane_at[0] : lane_at[0] + lane_at[1]
                ] = jnp.zeros((row_at[1], lane_at[1]), BF16)

    for step_x, step_y, copy in copies:

        @pl.when(inside(-step_x, -step_y))
        def _(copy=copy):
            copy.wait_recv()

    for step_x, step_y, copy in copies:

        @pl.when(inside(step_x, step_y))
        def _(copy=copy):
            copy.wait_send()


def halo(blocks, sizes, counts, collective):
    outs = [
        jax.ShapeDtypeStruct((b.shape[0] + 2 * r, b.shape[1] + 2 * l), b.dtype)
        for b, (r, l) in zip(blocks, sizes)
    ]
    scratch = [pltpu.SemaphoreType.DMA((8, len(sizes))), pltpu.SemaphoreType.DMA((8, len(sizes)))]
    return call(
        functools.partial(halo_kernel, sizes, counts),
        blocks, outs, scratch, "halo%d" % collective, collective,
    )


def sum_kernel(chunk, counts, x_ref, full, r1, s1, r2, s2, r3, send, recv):
    n_x, n_y = counts
    n_z = n_x // 2
    me_x, me_y = lax.axis_index("gx"), lax.axis_index("gy")
    core, me_z = lax.rem(me_x, 2), me_x // 2
    mid, half = chunk * n_z, chunk * n_z * n_y
    twin = (me_z * 2 + 1 - core, me_y)

    def y_peer(step):
        return lax.rem(me_y + step, n_y)

    def z_peer(step):
        return lax.rem(me_z + step, n_z)

    def y_place(step):
        return (me_x, y_peer(step))

    def z_place(step):
        return (z_peer(step) * 2 + core, me_y)

    barrier = pltpu.get_barrier_semaphore()
    peers = [twin] + [y_place(k) for k in range(1, n_y)] + [z_place(k) for k in range(1, n_z)]
    for peer in peers:
        pl.semaphore_signal(barrier, inc=1, device_id=peer, device_id_type=MESH)
    pl.semaphore_wait(barrier, len(peers))

    def copy(src, dst, at, place):
        made = pltpu.make_async_remote_copy(
            src_ref=src, dst_ref=dst, send_sem=send.at[at], recv_sem=recv.at[at],
            device_id=place, device_id_type=MESH,
        )
        made.start()
        return made

    def rows(start, size):
        return pl.ds(pl.multiple_of(start, 16), size)

    started = []
    count = 0
    mine = core * half
    one = copy(x_ref.at[rows((1 - core) * half, half)], r1, 0, twin)
    one.wait_recv()
    started.append(one)
    s1[...] = (x_ref[rows(mine, half), :].astype(F32) + r1[...].astype(F32)).astype(BF16)
    count = 1
    group = []
    for k in range(1, n_y):
        group.append(copy(s1.at[rows(y_peer(k) * mid, mid)], r2.at[k - 1], count, y_place(k)))
        count += 1
    total = s1[rows(me_y * mid, mid), :].astype(F32)
    for k, made in enumerate(group):
        made.wait_recv()
        total = total + r2[k].astype(F32)
    s2[...] = total.astype(BF16)
    started += group
    group = []
    for k in range(1, n_z):
        group.append(copy(s2.at[rows(z_peer(k) * chunk, chunk)], r3.at[k - 1], count, z_place(k)))
        count += 1
    total = s2[rows(me_z * chunk, chunk), :].astype(F32)
    for k, made in enumerate(group):
        made.wait_recv()
        total = total + r3[k].astype(F32)
    started += group
    base = mine + me_y * mid
    own = rows(base + me_z * chunk, chunk)
    full[own, :] = total.astype(BF16)
    group = []
    for k in range(1, n_z):
        group.append(copy(full.at[own], full.at[own], count, z_place(k)))
        count += 1
    for made in group:
        made.wait_recv()
    started += group
    own = rows(base, mid)
    group = []
    for k in range(1, n_y):
        group.append(copy(full.at[own], full.at[own], count, y_place(k)))
        count += 1
    for made in group:
        made.wait_recv()
    started += group
    own = rows(mine, half)
    last = copy(full.at[own], full.at[own], count, twin)
    last.wait_recv()
    started.append(last)
    for made in started:
        made.wait_send()


def sum_all(packed, chunk, counts, collective):
    n_x, n_y = counts
    n_z = n_x // 2
    copies = 2 + 2 * (n_y - 1) + 2 * (n_z - 1)
    half, mid = chunk * n_z * n_y, chunk * n_z
    scratch = [
        pltpu.VMEM((half, LANES), BF16),
        pltpu.VMEM((half, LANES), BF16),
        pltpu.VMEM((max(n_y - 1, 1), mid, LANES), BF16),
        pltpu.VMEM((mid, LANES), BF16),
        pltpu.VMEM((max(n_z - 1, 1), chunk, LANES), BF16),
        pltpu.SemaphoreType.DMA((copies,)),
        pltpu.SemaphoreType.DMA((copies,)),
    ]
    return call(
        functools.partial(sum_kernel, chunk, counts),
        [packed], [jax.ShapeDtypeStruct(packed.shape, BF16)], scratch, "sum_all", collective,
    )[0]


def parity_matrix(size, inverse):
    first = lax.broadcasted_iota(jnp.int32, (size, size), 0)
    second = lax.broadcasted_iota(jnp.int32, (size, size), 1)
    if inverse:
        first, second = second, first
    half = size // 2
    wanted = jnp.where(second < half, 2 * second, 2 * (second - half) + 1)
    return jnp.where(first == wanted, 1.0, 0.0).astype(BF16)


def moved(block, forward):
    lanes = block.shape[1]
    at = lax.broadcasted_iota(jnp.int32, block.shape, 1)
    turned = pltpu.roll(block.astype(F32), 1 if forward else lanes - 1, 1)
    return jnp.where(at == (0 if forward else lanes - 1), 0.0, turned).astype(BF16)


def fine_shifts(source, target):
    rows, lanes = source.shape
    half = LANES
    size = 2 * half
    def step(x, _):
        base = pl.multiple_of(x * size, size)
        even = source[:, pl.ds(base, half)]
        odd = source[:, pl.ds(base + half, half)]
        target[0:rows, pl.ds(base, half)] = moved(odd, True)
        target[0:rows, pl.ds(base + half, half)] = even
        target[rows : 2 * rows, pl.ds(base, half)] = even
        target[rows : 2 * rows, pl.ds(base + half, half)] = odd
        target[2 * rows : 3 * rows, pl.ds(base, half)] = odd
        target[2 * rows : 3 * rows, pl.ds(base + half, half)] = moved(even, False)
        return 0
    lax.fori_loop(0, lanes // size, step, 0)


def coarse_shifts(source, target):
    rows, lanes = source.shape
    for x in range(lanes // LANES):
        block = source[:, x * LANES : (x + 1) * LANES]
        target[0:rows, x * LANES : (x + 1) * LANES] = moved(block, True)
        target[rows : 2 * rows, x * LANES : (x + 1) * LANES] = block
        target[2 * rows : 3 * rows, x * LANES : (x + 1) * LANES] = moved(block, False)


def fine_conv(shifted, weight, store):
    size = 2 * LANES
    def step(x, _):
        total = None
        for along_x in range(3):
            base = pl.multiple_of((x + along_x) * size, size)
            term = dot(weight[along_x], shifted[:, pl.ds(base, size)])
            total = term if total is None else total + term
        store(pl.ds(pl.multiple_of(x * size, size), size), total)
        return 0
    lax.fori_loop(0, shifted.shape[1] // size - 2, step, 0)


def coarse_conv(shifted, weight):
    width = shifted.shape[1] - 2 * LANES
    total = None
    for along_x in range(3):
        term = dot(weight[along_x], shifted[:, along_x * LANES : along_x * LANES + width])
        total = term if total is None else total + term
    return total


def cells(n_qx, n_qy):
    found = []
    for a in range(2):
        for c in range(2):
            for qy in range(n_qy):
                for qx in range(n_qx):
                    found.append((2 * a + c, qy * n_qx + qx, qy, (2 * qx + a) * 2 + c))
    return found


def part(row, lane):
    return (slice(row * LANES, (row + 1) * LANES), slice(lane * LANES, (lane + 1) * LANES))


def to_wide(value, n_qy, channels):
    return jnp.concatenate([value[q * channels : (q + 1) * channels] for q in range(n_qy)], axis=1)


def first_kernel(field, cotan, w_first, w_last_t, w_down, hidden, coarse, back_sum, field_z, cotan_z, work, cells_ref, shifted):
    size = 2 * LANES
    matrix = parity_matrix(size, False)
    blocks = field.shape[1] // size
    for x in range(blocks):
        field_z[:, x * size : (x + 1) * size] = dot(field[:, x * size : (x + 1) * size], matrix).astype(BF16)
        work[:, x * size : (x + 1) * size] = dot(cotan[:, x * size : (x + 1) * size], matrix).astype(BF16)
    fine_shifts(field_z, shifted)

    def store_hidden(where, value):
        hidden[:, where] = leaky(value).astype(BF16)

    fine_conv(shifted, w_first, store_hidden)
    n_qx, n_qy = (blocks - 2) // 2, hidden.shape[0] // LANES
    for row, lane, fine_row, fine_lane in cells(n_qx, n_qy):
        cells_ref[part(row, lane)] = hidden[part(fine_row, fine_lane)]
    value = leaky(dot(w_down[...], cells_ref[...])).astype(BF16)
    width = n_qx * LANES
    for qy in range(n_qy):
        coarse[qy * LANES : (qy + 1) * LANES, :] = value[:, qy * width : (qy + 1) * width]
    rim = (work.shape[0] - hidden.shape[0]) // 2
    cotan_z[...] = work[rim : rim + hidden.shape[0], size : size + hidden.shape[1]]
    fine_shifts(work, shifted)

    def store_back(where, value):
        back_sum[:, where] = value

    fine_conv(shifted, w_last_t, store_back)


def level_kernel(coarse, w_coarse, w_up, w_up_t, hidden, back_sum, summed, back_level, grad_up, raised, back_cells, shifted):
    coarse_shifts(coarse, shifted)
    n_qx, n_qy = coarse.shape[1] // LANES - 2, coarse.shape[0] // LANES - 2
    level = to_wide(leaky(coarse_conv(shifted, w_coarse)).astype(BF16), n_qy, LANES)
    raised[...] = dot(w_up[...], level)
    for row, lane, fine_row, fine_lane in cells(n_qx, n_qy):
        here, fine = part(row, lane), part(fine_row, fine_lane)
        value = raised[here]
        root = lax.rsqrt(value * value + 1.0)
        summed[fine] = (leaky(value) + hidden[fine].astype(F32)).astype(BF16)
        back_cells[here] = (back_sum[fine] * (0.505 + 0.495 * value * root)).astype(BF16)
    grad_up[...] = dot_nt(back_cells[...], level)
    back = (dot(w_up_t[...], back_cells[...]) * slope_of(level)).astype(BF16)
    width = n_qx * LANES
    for qy in range(n_qy):
        back_level[qy * LANES : (qy + 1) * LANES, :] = back[:, qy * width : (qy + 1) * width]


def last_kernel(summed, back_level, coarse, hidden, back_sum, field_z, cotan_z, grad_up, w_last, w_coarse_t, w_down_t, output, packed, shifted, shifted_c, back_first, cells_ref, spread, total_ref):
    size = 2 * LANES
    matrix = parity_matrix(size, True)
    packed[...] = jnp.zeros(packed.shape, BF16)
    channels = 64
    n_y = hidden.shape[0] // channels
    n_qx, n_qy = coarse.shape[1] // LANES - 2, coarse.shape[0] // LANES - 2
    width = n_qx * LANES
    fine_rows = summed.shape[0]
    coarse_rows = coarse.shape[0]
    lanes = hidden.shape[1]
    in_half = lax.broadcasted_iota(jnp.int32, (channels, LANES), 1) < channels

    coarse_shifts(back_level, shifted_c)
    center = coarse[LANES : LANES * (1 + n_qy), LANES : LANES + width]
    back = (coarse_conv(shifted_c, w_coarse_t) * slope_of(center)).astype(BF16)
    back_wide = to_wide(back, n_qy, LANES)
    spread[...] = dot(w_down_t[...], back_wide)
    for row, lane, fine_row, fine_lane in cells(n_qx, n_qy):
        here, fine = part(row, lane), part(fine_row, fine_lane)
        mine = hidden[fine]
        cells_ref[here] = mine
        back_first[fine] = ((back_sum[fine] + spread[here]) * slope_of(mine)).astype(BF16)

    base = 27 * channels
    coarse_shifts(coarse, shifted_c)
    center = back_level[LANES : LANES * (1 + n_qy), LANES : LANES + width]
    for along_x in range(3):
        total_ref[:, : 3 * coarse_rows] = dot_nt(center, shifted_c[:, along_x * LANES : along_x * LANES + width])
        for along_z in range(3):
            for along_y in range(3):
                term = None
                for qy in range(n_qy):
                    lane = along_z * coarse_rows + (qy + along_y) * LANES
                    here = total_ref[qy * LANES : (qy + 1) * LANES, lane : lane + LANES]
                    term = here if term is None else term + here
                at = base + (along_x * 9 + along_y * 3 + along_z) * LANES
                packed[at : at + LANES, :] = term.astype(BF16)
    base = base + 27 * LANES
    for k in range(8):
        packed[base + k * 64 : base + k * 64 + 64, :] = grad_up[k * 64 : k * 64 + 64, :].astype(BF16)
    base = base + 512
    down = dot_nt(back_wide, cells_ref[...])
    for k in range(4):
        packed[base + k * LANES : base + (k + 1) * LANES, :] = down[:, k * LANES : (k + 1) * LANES].astype(BF16)

    def weight_grad(left, second):
        for along_x in range(3):
            total_ref[:, : 3 * fine_rows] = dot_nt(left[...], shifted[:, along_x * size : along_x * size + lanes])
            for along_z in range(3):
                total = None
                for y in range(n_y):
                    term = total_ref[y * channels : (y + 1) * channels, along_z * fine_rows : (along_z + 1) * fine_rows]
                    if y > 0:
                        term = pltpu.roll(term, fine_rows - channels * y, 1)
                    term = term[:, : 2 * LANES]
                    total = term if total is None else total + term
                at = (along_x * 3 + along_z) * 3 * channels
                tail = at + 2 * channels
                head = total[:, :LANES].astype(BF16)
                rest = total[:, LANES:]
                if second:
                    packed[at + channels : at + 2 * channels, :] = head
                    rest = pltpu.roll(rest, channels, 1)
                    packed[tail : tail + channels, :] = jnp.where(
                        in_half, packed[tail : tail + channels, :].astype(F32), rest
                    ).astype(BF16)
                else:
                    packed[at : at + channels, :] = head
                    packed[tail : tail + channels, :] = rest.astype(BF16)

    fine_shifts(field_z, shifted)
    weight_grad(back_first, False)
    fine_shifts(summed, shifted)
    weight_grad(cotan_z, True)

    def store(where, value):
        output[:, where] = dot(value.astype(BF16), matrix).astype(BF16)

    fine_conv(shifted, w_last, store)


def banded(weight, n_y, flipped):
    outer = weight.shape[0]
    taps = weight.reshape(outer, 3, 3, 3, -1)
    if flipped:
        taps = jnp.transpose(taps[:, ::-1, ::-1, ::-1], (1, 4, 3, 2, 0))
    else:
        taps = jnp.transpose(taps, (1, 0, 3, 2, 4))
    inner = taps.shape[-1]
    taps = taps.reshape(3, taps.shape[1], 3, 3 * inner)
    bands = [
        jnp.pad(taps, ((0, 0), (0, 0), (0, 0), (y * inner, (n_y - 1 - y) * inner)))
        for y in range(n_y)
    ]
    return jnp.stack(bands, axis=1).reshape(3, n_y * taps.shape[1], 3 * (n_y + 2) * inner)


def shards(counts, field, weight_first, weight_down, weight_coarse, weight_up, weight_last, cotangent):
    channels, size_x, size_y, size_z = field.shape
    wide = weight_down.shape[0]
    n_qx, n_qy = size_x // 2, size_y // 2
    rows, lanes = size_y * channels, size_x * size_z
    fine = lambda v: jnp.transpose(v, (2, 0, 1, 3)).reshape(rows, lanes)
    shape = jax.ShapeDtypeStruct

    w_first = banded(weight_first, size_y, False)
    w_last = banded(weight_last, size_y, False)
    w_last_t = banded(weight_last, size_y, True)
    w_coarse = banded(weight_coarse, n_qy, False)
    w_coarse_t = banded(weight_coarse, n_qy, True)
    w_down = jnp.transpose(weight_down.reshape(wide, 2, 2, 2, channels), (0, 1, 3, 2, 4)).reshape(wide, 8 * channels)
    w_up = jnp.transpose(weight_up.reshape(channels, 2, 2, 2, wide), (1, 3, 2, 0, 4)).reshape(8 * channels, wide)

    fine_rim, coarse_rim = (channels, size_z), (wide, size_z // 2)
    field_w, cotan_w = halo([fine(field), fine(cotangent)], [fine_rim, fine_rim], counts, 0)
    full_rows, full_lanes = field_w.shape
    n_cells = n_qx * n_qy * LANES
    hidden, coarse, back_sum, field_z, cotan_z = call(
        first_kernel,
        [field_w, cotan_w, w_first, w_last_t, w_down],
        [
            shape((rows, lanes), BF16),
            shape((n_qy * wide, n_qx * LANES), BF16),
            shape((rows, lanes), F32),
            shape((full_rows, full_lanes), BF16),
            shape((rows, lanes), BF16),
        ],
        [
            pltpu.VMEM((full_rows, full_lanes), BF16),
            pltpu.VMEM((8 * channels, n_cells), BF16),
            pltpu.VMEM((3 * full_rows, full_lanes), BF16),
        ],
        "first",
    )
    (coarse_w,) = halo([coarse], [coarse_rim], counts, 1)
    coarse_rows, coarse_lanes = coarse_w.shape
    summed, back_level, grad_up = call(
        level_kernel,
        [coarse_w, w_coarse, w_up, w_up.T, hidden, back_sum],
        [
            shape((rows, lanes), BF16),
            shape((n_qy * wide, n_qx * LANES), BF16),
            shape((8 * channels, wide), F32),
        ],
        [
            pltpu.VMEM((8 * channels, n_cells), F32),
            pltpu.VMEM((8 * channels, n_cells), BF16),
            pltpu.VMEM((3 * coarse_rows, coarse_lanes), BF16),
        ],
        "level",
    )
    summed_w, back_level_w = halo([summed, back_level], [fine_rim, coarse_rim], counts, 2)
    used = 27 * channels + 27 * wide + 8 * channels + 4 * wide
    devices = counts[0] * counts[1]
    chunk = -(-used // (devices * 16)) * 16
    output, packed = call(
        last_kernel,
        [summed_w, back_level_w, coarse_w, hidden, back_sum, field_z, cotan_z, grad_up, w_last, w_coarse_t, w_down.T],
        [shape((rows, lanes), BF16), shape((chunk * devices, LANES), BF16)],
        [
            pltpu.VMEM((3 * full_rows, full_lanes), BF16),
            pltpu.VMEM((3 * coarse_rows, coarse_lanes), BF16),
            pltpu.VMEM((rows, lanes), BF16),
            pltpu.VMEM((8 * channels, n_cells), BF16),
            pltpu.VMEM((8 * channels, n_cells), F32),
            pltpu.VMEM((max(rows, n_qy * wide), 3 * max(full_rows, coarse_rows)), F32),
        ],
        "last",
    )
    sums = sum_all(packed, chunk, counts, 3).astype(F32)
    at = 27 * channels
    both = sums[:at].reshape(3, 3, 3, channels, LANES)

    def fine_grad(head, tail):
        units = jnp.concatenate([head, tail], axis=-1).reshape(3, 3, channels, 3, channels)
        return jnp.transpose(units, (2, 0, 3, 1, 4)).reshape(channels, 27 * channels)

    grad_first = fine_grad(both[:, :, 0], both[:, :, 2, :, :channels])
    grad_last = fine_grad(both[:, :, 1], both[:, :, 2, :, channels:])
    grad_coarse = jnp.transpose(sums[at : at + 27 * wide].reshape(27, wide, wide), (1, 0, 2)).reshape(wide, 27 * wide)
    at += 27 * wide
    grad_up = jnp.transpose(
        sums[at : at + 8 * channels].reshape(2, 2, 2, channels, wide), (3, 0, 2, 1, 4)
    ).reshape(channels, 8 * wide)
    at += 8 * channels
    grad_down = jnp.transpose(
        sums[at : at + 4 * wide].reshape(2, 2, wide, 2, channels), (2, 0, 3, 1, 4)
    ).reshape(wide, 8 * channels)
    output = jnp.transpose(output.reshape(size_y, channels, size_x, size_z), (1, 2, 0, 3))
    return (output, grad_first, grad_down, grad_coarse, grad_up, grad_last)


def solution(mesh):
    counts = (mesh.shape["gx"], mesh.shape["gy"])
    in_specs = (P(None, "gx", "gy", None), P(), P(), P(), P(), P(), P(None, "gx", "gy", None))
    out_specs = (P(None, "gx", "gy", None), P(), P(), P(), P(), P())
    return jax.shard_map(
        functools.partial(shards, counts), mesh=mesh, in_specs=in_specs, out_specs=out_specs, check_vma=False
    )
```

profile of v0, /device:TPU:0, one launch (start us, length us, event | category | flops | bytes accessed | tf_op | source)
XLA Modules:
  0.0 220.5 jit_solution(7711854219488921940)
XLA Ops:
  0.6 1.5 reshape.112
  2.2 1.7 rev.6
  5.8 3.6 %copy.78 = bf16[3,4,64,3,384]{4,3,2,1,0:T(4,128)(2,1)} copy(bf16[3,4,64,3,384]{2,4,3,0,1:T(8,128)(2,1)S(1)} %pad_maximum_fusion.1) | data formatting | bytes 3538944 | tf_op jit(solution)/shard_map/stack | solution.py:483
  9.5 5.4 %reshape.114.w_last_t = bf16[3,256,1152]{2,1,0:T(8,128)(2,1)} reshape(bf16[3,4,64,3,384]{4,3,2,1,0:T(4,128)(2,1)} %copy.78) | data formatting | bytes 3538944 | tf_op jit(solution)/shard_map/reshape | solution.py:483
  18.0 3.6 %copy.76 = bf16[3,4,64,3,384]{4,3,2,1,0:T(4,128)(2,1)} copy(bf16[3,4,64,3,384]{2,4,3,0,1:T(8,128)(2,1)S(1)} %pad_maximum_fusion) | data formatting | bytes 3538944 | tf_op jit(solution)/shard_map/stack | solution.py:483
  21.6 5.4 %reshape.111.w_first = bf16[3,256,1152]{2,1,0:T(8,128)(2,1)} reshape(bf16[3,4,64,3,384]{4,3,2,1,0:T(4,128)(2,1)} %copy.76) | data formatting | bytes 3538944 | tf_op jit(solution)/shard_map/reshape | solution.py:483
  29.3 15.5 %halo0.1 = (bf16[384,1536]{1,0:T(8,128)(2,1)}, bf16[384,1536]{1,0:T(8,128)(2,1)}) custom-call(bf16[256,1024]{1,0:T(8,128)(2,1)} %bitcast.102, bf16[256,1024]{1,0:T(8,128)(2,1)} %bitcast.103), custom_call_target="tpu_custom_call" | custom-call | tf_op jit(solution)/shard_map/halo0/pallas_call | solution.py:38
  45.8 12.8 %first.1 = (bf16[256,1024]{1,0:T(8,128)(2,1)}, bf16[256,256]{1,0:T(8,128)(2,1)}, f32[256,1024]{1,0:T(8,128)}, bf16[384,1536]{1,0:T(8,128)(2,1)}, bf16[256,1024]{1,0:T(8,128)(2,1)}) custom-call(bf16[384,1536]{1,0:T(8,128)(2,1)} %get-tuple-element.20.field, bf16[384,1536]{1,0:T(8,128)(2,1)} %get-tuple-element.21.cotan, ...), custom_call_target="tpu_custom_call" | custom-call | tf_op jit(solution)/shard_map/first/pallas_call | solution.py:38
  58.6 15.8 %halo1.1.coarse = bf16[512,512]{1,0:T(8,128)(2,1)} custom-call(bf16[256,256]{1,0:T(8,128)(2,1)} %get-tuple-element.22.refs_0_), custom_call_target="tpu_custom_call" | custom-call | tf_op jit(solution)/shard_map/halo1/pallas_call | solution.py:38
  74.4 1.0 copy.82
  76.4 1.6 pad_maximum_fusion.3
  78.0 4.7 %copy.106 = bf16[3,2,128,3,512]{4,3,2,1,0:T(4,128)(2,1)S(1)} copy(bf16[3,2,128,3,512]{2,4,3,0,1:T(8,128)(2,1)} %pad_maximum_fusion.3) | data formatting | bytes 4718592 | tf_op jit(solution)/shard_map/reshape | solution.py:483
  82.7 4.9 %reshape.138.w_coarse = bf16[3,256,1536]{2,1,0:T(8,128)(2,1)} reshape(bf16[3,2,128,3,512]{4,3,2,1,0:T(4,128)(2,1)S(1)} %copy.106) | data formatting | bytes 4718592 | tf_op jit(solution)/shard_map/reshape | solution.py:483
  88.5 5.6 %level.1 = (bf16[256,1024]{1,0:T(8,128)(2,1)}, bf16[256,256]{1,0:T(8,128)(2,1)}, f32[512,128]{1,0:T(8,128)}) custom-call(bf16[512,512]{1,0:T(8,128)(2,1)} %halo1.1.coarse, bf16[3,256,1536]{2,1,0:T(8,128)(2,1)} %reshape.138.w_coarse, bf16[512,128]{1,0:T(8,128)(2,1)} %bitcast.114, bf16[128,512]{1,0:T(8,128)(2,1)} %bitcast.118, ...), custom_call_target="tpu_custom_call" | custom-call | tf_op jit(solution)/shard_map/level/pallas_call | solution.py:38
  94.1 13.9 %halo2.1 = (bf16[384,1536]{1,0:T(8,128)(2,1)}, bf16[512,512]{1,0:T(8,128)(2,1)}) custom-call(bf16[256,1024]{1,0:T(8,128)(2,1)} %get-tuple-element.25.refs_0_, bf16[256,256]{1,0:T(8,128)(2,1)} %get-tuple-element.26.refs_1_), custom_call_target="tpu_custom_call" | custom-call | tf_op jit(solution)/shard_map/halo2/pallas_call | solution.py:38
  110.8 3.7 %copy.89 = bf16[3,4,64,3,384]{4,3,2,1,0:T(4,128)(2,1)} copy(bf16[3,4,64,3,384]{2,4,3,0,1:T(8,128)(2,1)S(1)} %pad_maximum_fusion.2) | data formatting | bytes 3538944 | tf_op jit(solution)/shard_map/stack | solution.py:483
  114.5 5.4 %reshape.123.w_last = bf16[3,256,1152]{2,1,0:T(8,128)(2,1)} reshape(bf16[3,4,64,3,384]{4,3,2,1,0:T(4,128)(2,1)} %copy.89) | data formatting | bytes 3538944 | tf_op jit(solution)/shard_map/reshape | solution.py:483
  120.0 1.4 copy.90
  121.7 1.6 pad_maximum_fusion.4
  123.4 4.7 %copy.107 = bf16[3,2,128,3,512]{4,3,2,1,0:T(4,128)(2,1)S(1)} copy(bf16[3,2,128,3,512]{2,4,3,0,1:T(8,128)(2,1)} %pad_maximum_fusion.4) | data formatting | bytes 4718592 | tf_op jit(solution)/shard_map/reshape | solution.py:483
  128.0 4.9 %reshape.139.w_coarse_t = bf16[3,256,1536]{2,1,0:T(8,128)(2,1)} reshape(bf16[3,2,128,3,512]{4,3,2,1,0:T(4,128)(2,1)S(1)} %copy.107) | data formatting | bytes 4718592 | tf_op jit(solution)/shard_map/reshape | solution.py:483
  133.0 18.9 %last.1 = (bf16[256,1024]{1,0:T(8,128)(2,1)}, bf16[6656,128]{1,0:T(8,128)(2,1)}) custom-call(bf16[384,1536]{1,0:T(8,128)(2,1)} %get-tuple-element.27.summed, bf16[512,512]{1,0:T(8,128)(2,1)} %get-tuple-element.28.back_level, bf16[512,512]{1,0:T(8,128)(2,1)} %halo1.1.coarse, bf16[256,1024]{1,0:T(8,128)(2,1)} %get-tuple-element.23.hidden, ...), custom_call_target="tpu_custom_call" | custom-call | tf_op jit(solution)/shard_map/last/pallas_call | solution.py:38
  151.9 50.4 %sum_all.1 = bf16[6656,128]{1,0:T(8,128)(2,1)} custom-call(bf16[6656,128]{1,0:T(8,128)(2,1)} %get-tuple-element.33.x_ref), custom_call_target="tpu_custom_call" | custom-call | tf_op jit(solution)/shard_map/sum_all/pallas_call | solution.py:38
  202.2 1.1 slice.32
  204.0 1.0 copy.103
  205.0 1.3 reshape.137
  207.7 1.9 copy.96
  209.6 1.3 reshape.129
  210.9 1.3 slice.36
  212.2 2.2 copy.99
  214.4 1.9 copy.105
  219.0 1.5 copy.117
  (68 shorter events, 17.7 us)
Async XLA Ops:
  2.2 2.7 %copy-start.3 = (bf16[64,3,3,3,64]{4,3,2,1,0:T(4,128)(2,1)}, bf16[64,3,3,3,64]{4,3,2,1,0:T(4,128)(2,1)S(1)}, u32[]{:S(2)}) copy-start(bf16[64,3,3,3,64]{4,3,2,1,0:T(4,128)(2,1)S(1)} %reshape.112) | copy-start | bytes 663556
  9.5 5.4 %copy-start.11 = (bf16[64,1728]{1,0:T(8,128)(2,1)S(1)}, bf16[64,1728]{1,0:T(8,128)(2,1)}, u32[]{:S(2)}) copy-start(bf16[64,1728]{1,0:T(8,128)(2,1)} %param.8) | copy-start | bytes 663556
  21.6 5.4 %copy-start.8 = (bf16[64,4,4,256]{3,2,1,0:T(4,128)(2,1)S(1)}, bf16[64,4,4,256]{3,2,1,0:T(4,128)(2,1)}, u32[]{:S(2)}) copy-start(bf16[64,4,4,256]{3,2,1,0:T(4,128)(2,1)} %param.7) | copy-start | bytes 1572868
  21.6 6.6 %copy-start.9 = (bf16[64,4,4,256]{3,2,1,0:T(4,128)(2,1)S(1)}, bf16[64,4,4,256]{3,2,1,0:T(4,128)(2,1)}, u32[]{:S(2)}) copy-start(bf16[64,4,4,256]{3,2,1,0:T(4,128)(2,1)} %param.13) | copy-start | bytes 1572868
  27.3 17.6 %copy-start.12 = (bf16[128,512]{1,0:T(8,128)(2,1)S(1)}, bf16[128,512]{1,0:T(8,128)(2,1)}, u32[]{:S(2)}) copy-start(bf16[128,512]{1,0:T(8,128)(2,1)} %param.9) | copy-start | bytes 393220
  45.0 13.6 %copy-start.5 = (bf16[128,2,2,2,64]{0,4,3,2,1:T(8,128)(2,1)}, bf16[128,2,2,2,64]{0,4,3,2,1:T(8,128)(2,1)S(1)}, u32[]{:S(2)}) copy-start(bf16[128,2,2,2,64]{0,4,3,2,1:T(8,128)(2,1)S(1)} %copy.80) | copy-start | bytes 393220
  45.8 28.6 %copy-start.7 = (bf16[128,3456]{1,0:T(8,128)(2,1)S(1)}, bf16[128,3456]{1,0:T(8,128)(2,1)}, u32[]{:S(2)}) copy-start(bf16[128,3456]{1,0:T(8,128)(2,1)} %param.10) | copy-start | bytes 2654212
  75.4 0.9 copy-start.1
  82.7 5.0 %copy-start.13 = (bf16[64,1024]{1,0:T(8,128)(2,1)S(1)}, bf16[64,1024]{1,0:T(8,128)(2,1)}, u32[]{:S(2)}) copy-start(bf16[64,1024]{1,0:T(8,128)(2,1)} %param.11) | copy-start | bytes 393220
  87.7 0.8 copy-start.6
  88.5 19.5 %copy-start.4 = (bf16[64,3,3,3,64]{4,3,2,1,0:T(4,128)(2,1)S(1)}, bf16[64,3,3,3,64]{4,3,2,1,0:T(4,128)(2,1)}, u32[]{:S(2)}) copy-start(bf16[64,3,3,3,64]{4,3,2,1,0:T(4,128)(2,1)} %copy-done.3) | copy-start | bytes 663556
  114.5 5.4 %copy-start.2 = (bf16[128,3456]{0,1:T(8,128)(2,1)S(1)}, bf16[128,3456]{0,1:T(8,128)(2,1)}, u32[]{:S(2)}) copy-start(bf16[128,3456]{0,1:T(8,128)(2,1)} %copy-done.1) | copy-start | bytes 2654212
  206.7 4.2 %copy-start = (bf16[6656,128]{1,0:T(8,128)(2,1)S(1)}, bf16[6656,128]{1,0:T(8,128)(2,1)}, u32[]{:S(2)}) copy-start(bf16[6656,128]{1,0:T(8,128)(2,1)} %sum_all.1) | copy-start | bytes 5111812
  216.3 2.3 %copy-start.10 = (bf16[256,1024]{1,0:T(8,128)(2,1)S(1)}, bf16[256,1024]{1,0:T(8,128)(2,1)}, u32[]{:S(2)}) copy-start(bf16[256,1024]{1,0:T(8,128)(2,1)} %get-tuple-element.32) | copy-start | bytes 1572868
where the time goes:
time: 223 us; the launch traced here: 220 us
  Pallas kernels  133 us (60%)
  local copies, waits for them, and re-layouts  79.3 us (36%)
  other arithmetic  7.24 us (3%)
    pallas_call x7, Pallas kernels, call(): pl.pallas_call(kernel, out_shape=outs, in_specs=[pl.BlockSpec(memory_spac...  133 us
    reshape x7, local copies, waits for them, and re-layouts, banded(): jnp.stack(bands, axis=1)  35.5 us
    another operation x8, local copies, waits for them, and re-layouts, banded(): jnp.stack(bands, axis=1)  14.1 us
    unnamed x38, local copies, waits for them, and re-layouts  6.98 us
    another operation x5, other arithmetic, banded(): jnp.stack(bands, axis=1)  6.18 us

commit v1 on v0

--- a/solution.py
+++ b/solution.py
@@ -337,8 +337,92 @@
     return jnp.concatenate([value[q * channels : (q + 1) * channels] for q in range(n_qy)], axis=1)
 
 
-def first_kernel(field, cotan, w_first, w_last_t, w_down, hidden, coarse, back_sum, field_z, cotan_z, work, cells_ref, shifted):
+def left_half(shape):
+    return lax.broadcasted_iota(jnp.int32, shape, 1) < shape[1] // 2
+
+
+def band_fine(weight, twice, target, n_y, flipped):
+    channels = weight.shape[0]
+    left = left_half((channels, LANES))
+    for k in range(14):
+        block = weight[:, k * LANES : (k + 1) * LANES].astype(F32)
+        count = min(2, 27 - 2 * k)
+        if flipped:
+            both = jnp.concatenate([block, block], axis=0).T
+            twice[k * LANES : k * LANES + count * channels, :] = both[: count * channels]
+        else:
+            turned = pltpu.roll(block, channels, 1)
+            twice[k * LANES : k * LANES + channels, :] = jnp.where(left, block, turned)
+            if count == 2:
+                twice[k * LANES + channels : (k + 1) * LANES, :] = jnp.where(left, turned, block)
+    zero = jnp.zeros((channels, LANES), F32)
+    width = (n_y + 2) * channels
+    for along_x in range(3):
+        for along_z in range(3):
+
+            def unit(along_y):
+                if along_y < 0 or along_y > 2:
+                    return zero
+                tap = along_x * 9 + along_y * 3 + along_z
+                tap = 26 - tap if flipped else tap
+                return twice[tap * channels : (tap + 1) * channels, :]
+
+            for y in range(n_y):
+                for k in range(width // LANES):
+                    lane = along_z * width + k * LANES
+                    target[along_x, y * channels : (y + 1) * channels, lane : lane + LANES] = jnp.where(
+                        left, unit(2 * k - y), unit(2 * k + 1 - y)
+                    ).astype(BF16)
+
+
+def band_coarse(weight, target, n_y, flipped):
+    width = (n_y + 2) * LANES
+    for along_x in range(3):
+        for along_z in range(3):
+            for row in range(n_y + 2):
+                for y in range(n_y):
+                    if row - y < 0 or row - y > 2:
+                        lane = along_z * width + row * LANES
+                        target[along_x, y * LANES : (y + 1) * LANES, lane : lane + LANES] = jnp.zeros((LANES, LANES), BF16)
+            for along_y in range(3):
+                tap = along_x * 9 + along_y * 3 + along_z
+                tap = 26 - tap if flipped else tap
+                block = weight[:, tap * LANES : (tap + 1) * LANES]
+                if flipped:
+                    block = block.astype(F32).T.astype(BF16)
+                for y in range(n_y):
+                    lane = along_z * width + (y + along_y) * LANES
+                    target[along_x, y * LANES : (y + 1) * LANES, lane : lane + LANES] = block
+
+
+def down_weight(weight):
+    channels = LANES // 2
+    left = left_half((weight.shape[0], LANES))
+    pieces = []
+    for a in range(2):
+        zero = weight[:, 4 * a * channels : 4 * a * channels + LANES].astype(F32)
+        one = weight[:, (4 * a + 2) * channels : (4 * a + 2) * channels + LANES].astype(F32)
+        pieces.append(jnp.where(left, zero, pltpu.roll(one, channels, 1)))
+        pieces.append(jnp.where(left, pltpu.roll(zero, channels, 1), one))
+    return jnp.concatenate(pieces, axis=1)
+
+
+def up_weight(weight):
+    pieces = []
+    for a in range(2):
+        for c in range(2):
+            for b in range(2):
+                tap = 4 * a + 2 * b + c
+                pieces.append(weight[:, tap * LANES : (tap + 1) * LANES].astype(F32))
+    return jnp.concatenate(pieces, axis=0)
+
+
+def first_kernel(field, cotan, weight_first, weight_last, weight_down, hidden, coarse, back_sum, field_z, cotan_z, work, cells_ref, shifted, w_first, w_last_t, twice):
     size = 2 * LANES
+    n_y = hidden.shape[0] // weight_first.shape[0]
+    band_fine(weight_first, twice, w_first, n_y, False)
+    band_fine(weight_last, twice, w_last_t, n_y, True)
+    w_down = down_weight(weight_down).astype(BF16)
     matrix = parity_matrix(size, False)
     blocks = field.shape[1] // size
     for x in range(blocks):
@@ -353,7 +437,7 @@
     n_qx, n_qy = (blocks - 2) // 2, hidden.shape[0] // LANES
     for row, lane, fine_row, fine_lane in cells(n_qx, n_qy):
         cells_ref[part(row, lane)] = hidden[part(fine_row, fine_lane)]
-    value = leaky(dot(w_down[...], cells_ref[...])).astype(BF16)
+    value = leaky(dot(w_down, cells_ref[...])).astype(BF16)
     width = n_qx * LANES
     for qy in range(n_qy):
         coarse[qy * LANES : (qy + 1) * LANES, :] = value[:, qy * width : (qy + 1) * width]
@@ -367,11 +451,15 @@
     fine_conv(shifted, w_last_t, store_back)
 
 
-def level_kernel(coarse, w_coarse, w_up, w_up_t, hidden, back_sum, summed, back_level, grad_up, raised, back_cells, shifted):
+def level_kernel(coarse, weight_coarse, weight_up, hidden, back_sum, summed, back_level, grad_up, raised, back_cells, shifted, w_coarse):
     coarse_shifts(coarse, shifted)
     n_qx, n_qy = coarse.shape[1] // LANES - 2, coarse.shape[0] // LANES - 2
+    band_coarse(weight_coarse, w_coarse, n_qy, False)
+    w_up = up_weight(weight_up)
+    w_up_t = w_up.T.astype(BF16)
+    w_up = w_up.astype(BF16)
     level = to_wide(leaky(coarse_conv(shifted, w_coarse)).astype(BF16), n_qy, LANES)
-    raised[...] = dot(w_up[...], level)
+    raised[...] = dot(w_up, level)
     for row, lane, fine_row, fine_lane in cells(n_qx, n_qy):
         here, fine = part(row, lane), part(fine_row, fine_lane)
         value = raised[here]
@@ -379,13 +467,13 @@
         summed[fine] = (leaky(value) + hidden[fine].astype(F32)).astype(BF16)
         back_cells[here] = (back_sum[fine] * (0.505 + 0.495 * value * root)).astype(BF16)
     grad_up[...] = dot_nt(back_cells[...], level)
-    back = (dot(w_up_t[...], back_cells[...]) * slope_of(level)).astype(BF16)
+    back = (dot(w_up_t, back_cells[...]) * slope_of(level)).astype(BF16)
     width = n_qx * LANES
     for qy in range(n_qy):
         back_level[qy * LANES : (qy + 1) * LANES, :] = back[:, qy * width : (qy + 1) * width]
 
 
-def last_kernel(summed, back_level, coarse, hidden, back_sum, field_z, cotan_z, grad_up, w_last, w_coarse_t, w_down_t, output, packed, shifted, shifted_c, back_first, cells_ref, spread, total_ref):
+def last_kernel(summed, back_level, coarse, hidden, back_sum, field_z, cotan_z, grad_up, weight_last, weight_coarse, weight_down, output, packed, shifted, shifted_c, back_first, cells_ref, spread, total_ref, w_last, w_coarse_t, twice):
     size = 2 * LANES
     matrix = parity_matrix(size, True)
     packed[...] = jnp.zeros(packed.shape, BF16)
@@ -396,13 +484,16 @@
     fine_rows = summed.shape[0]
     coarse_rows = coarse.shape[0]
     lanes = hidden.shape[1]
-    in_half = lax.broadcasted_iota(jnp.int32, (channels, LANES), 1) < channels
+    in_half = left_half((channels, LANES))
+    band_fine(weight_last, twice, w_last, n_y, False)
+    band_coarse(weight_coarse, w_coarse_t, n_qy, True)
+    w_down_t = down_weight(weight_down).T.astype(BF16)
 
     coarse_shifts(back_level, shifted_c)
     center = coarse[LANES : LANES * (1 + n_qy), LANES : LANES + width]
     back = (coarse_conv(shifted_c, w_coarse_t) * slope_of(center)).astype(BF16)
     back_wide = to_wide(back, n_qy, LANES)
-    spread[...] = dot(w_down_t[...], back_wide)
+    spread[...] = dot(w_down_t, back_wide)
     for row, lane, fine_row, fine_lane in cells(n_qx, n_qy):
         here, fine = part(row, lane), part(fine_row, fine_lane)
         mine = hidden[fine]
@@ -467,20 +558,41 @@
     fine_conv(shifted, w_last, store)
 
 
-def banded(weight, n_y, flipped):
-    outer = weight.shape[0]
-    taps = weight.reshape(outer, 3, 3, 3, -1)
-    if flipped:
-        taps = jnp.transpose(taps[:, ::-1, ::-1, ::-1], (1, 4, 3, 2, 0))
-    else:
-        taps = jnp.transpose(taps, (1, 0, 3, 2, 4))
-    inner = taps.shape[-1]
-    taps = taps.reshape(3, taps.shape[1], 3, 3 * inner)
-    bands = [
-        jnp.pad(taps, ((0, 0), (0, 0), (0, 0), (y * inner, (n_y - 1 - y) * inner)))
-        for y in range(n_y)
-    ]
-    return jnp.stack(bands, axis=1).reshape(3, n_y * taps.shape[1], 3 * (n_y + 2) * inner)
+def unpack_kernel(sums, first, down, coarse, up, last):
+    channels = first.shape[0]
+    left = left_half((channels, LANES))
+
+    def piece(tap, which, side):
+        along_x, along_y, along_z = tap // 9, tap // 3 % 3, tap % 3
+        at = (along_x * 3 + along_z) * 3 * channels
+        at += 2 * channels if along_y == 2 else which * channels
+        held = which if along_y == 2 else along_y
+        value = sums[at : at + channels, :].astype(F32)
+        return value if held == side else pltpu.roll(value, channels, 1)
+
+    for which, target in ((0, first), (1, last)):
+        for k in range(13):
+            target[:, k * LANES : (k + 1) * LANES] = jnp.where(
+                left, piece(2 * k, which, 0), piece(2 * k + 1, which, 1)
+            )
+        target[:, 13 * LANES : 13 * LANES + channels] = piece(26, which, 0)[:, :channels]
+    at = 27 * channels
+    for k in range(27):
+        coarse[:, k * LANES : (k + 1) * LANES] = sums[at + k * LANES : at + (k + 1) * LANES, :].astype(F32)
+    at += 27 * LANES
+    for a in range(2):
+        for c in range(2):
+            for b in range(2):
+                tap, row = 4 * a + 2 * b + c, at + (4 * a + 2 * c + b) * channels
+                up[:, tap * LANES : (tap + 1) * LANES] = sums[row : row + channels, :].astype(F32)
+    at += 8 * channels
+    wide_left = left_half((LANES, LANES))
+    for a in range(2):
+        zero = sums[at + 2 * a * LANES : at + (2 * a + 1) * LANES, :].astype(F32)
+        one = sums[at + (2 * a + 1) * LANES : at + (2 * a + 2) * LANES, :].astype(F32)
+        base = 2 * a * LANES
+        down[:, base : base + LANES] = jnp.where(wide_left, zero, pltpu.roll(one, channels, 1))
+        down[:, base + LANES : base + 2 * LANES] = jnp.where(wide_left, pltpu.roll(zero, channels, 1), one)
 
 
 def shards(counts, field, weight_first, weight_down, weight_coarse, weight_up, weight_last, cotangent):
@@ -491,21 +603,15 @@
     fine = lambda v: jnp.transpose(v, (2, 0, 1, 3)).reshape(rows, lanes)
     shape = jax.ShapeDtypeStruct
 
-    w_first = banded(weight_first, size_y, False)
-    w_last = banded(weight_last, size_y, False)
-    w_last_t = banded(weight_last, size_y, True)
-    w_coarse = banded(weight_coarse, n_qy, False)
-    w_coarse_t = banded(weight_coarse, n_qy, True)
-    w_down = jnp.transpose(weight_down.reshape(wide, 2, 2, 2, channels), (0, 1, 3, 2, 4)).reshape(wide, 8 * channels)
-    w_up = jnp.transpose(weight_up.reshape(channels, 2, 2, 2, wide), (1, 3, 2, 0, 4)).reshape(8 * channels, wide)
-
+    whole = lambda v: jnp.pad(v, ((0, 0), (0, channels)))
+    weight_first, weight_last = whole(weight_first), whole(weight_last)
     fine_rim, coarse_rim = (channels, size_z), (wide, size_z // 2)
     field_w, cotan_w = halo([fine(field), fine(cotangent)], [fine_rim, fine_rim], counts, 0)
     full_rows, full_lanes = field_w.shape
     n_cells = n_qx * n_qy * LANES
     hidden, coarse, back_sum, field_z, cotan_z = call(
         first_kernel,
-        [field_w, cotan_w, w_first, w_last_t, w_down],
+        [field_w, cotan_w, weight_first, weight_last, weight_down],
         [
             shape((rows, lanes), BF16),
             shape((n_qy * wide, n_qx * LANES), BF16),
@@ -517,6 +623,9 @@
             pltpu.VMEM((full_rows, full_lanes), BF16),
             pltpu.VMEM((8 * channels, n_cells), BF16),
             pltpu.VMEM((3 * full_rows, full_lanes), BF16),
+            pltpu.VMEM((3, rows, 3 * full_rows), BF16),
+            pltpu.VMEM((3, rows, 3 * full_rows), BF16),
+            pltpu.VMEM((27 * channels, LANES), F32),
         ],
         "first",
     )
@@ -524,7 +633,7 @@
     coarse_rows, coarse_lanes = coarse_w.shape
     summed, back_level, grad_up = call(
         level_kernel,
-        [coarse_w, w_coarse, w_up, w_up.T, hidden, back_sum],
+        [coarse_w, weight_coarse, weight_up, hidden, back_sum],
         [
             shape((rows, lanes), BF16),
             shape((n_qy * wide, n_qx * LANES), BF16),
@@ -534,6 +643,7 @@
             pltpu.VMEM((8 * channels, n_cells), F32),
             pltpu.VMEM((8 * channels, n_cells), BF16),
             pltpu.VMEM((3 * coarse_rows, coarse_lanes), BF16),
+            pltpu.VMEM((3, n_qy * wide, 3 * coarse_rows), BF16),
         ],
         "level",
     )
@@ -543,7 +653,7 @@
     chunk = -(-used // (devices * 16)) * 16
     output, packed = call(
         last_kernel,
-        [summed_w, back_level_w, coarse_w, hidden, back_sum, field_z, cotan_z, grad_up, w_last, w_coarse_t, w_down.T],
+        [summed_w, back_level_w, coarse_w, hidden, back_sum, field_z, cotan_z, grad_up, weight_last, weight_coarse, weight_down],
         [shape((rows, lanes), BF16), shape((chunk * devices, LANES), BF16)],
         [
             pltpu.VMEM((3 * full_rows, full_lanes), BF16),
@@ -552,28 +662,26 @@
             pltpu.VMEM((8 * channels, n_cells), BF16),
             pltpu.VMEM((8 * channels, n_cells), F32),
             pltpu.VMEM((max(rows, n_qy * wide), 3 * max(full_rows, coarse_rows)), F32),
+            pltpu.VMEM((3, rows, 3 * full_rows), BF16),
+            pltpu.VMEM((3, n_qy * wide, 3 * coarse_rows), BF16),
+            pltpu.VMEM((27 * channels, LANES), F32),
         ],
         "last",
     )
-    sums = sum_all(packed, chunk, counts, 3).astype(F32)
-    at = 27 * channels
-    both = sums[:at].reshape(3, 3, 3, channels, LANES)
-
-    def fine_grad(head, tail):
-        units = jnp.concatenate([head, tail], axis=-1).reshape(3, 3, channels, 3, channels)
-        return jnp.transpose(units, (2, 0, 3, 1, 4)).reshape(channels, 27 * channels)
-
-    grad_first = fine_grad(both[:, :, 0], both[:, :, 2, :, :channels])
-    grad_last = fine_grad(both[:, :, 1], both[:, :, 2, :, channels:])
-    grad_coarse = jnp.transpose(sums[at : at + 27 * wide].reshape(27, wide, wide), (1, 0, 2)).reshape(wide, 27 * wide)
-    at += 27 * wide
-    grad_up = jnp.transpose(
-        sums[at : at + 8 * channels].reshape(2, 2, 2, channels, wide), (3, 0, 2, 1, 4)
-    ).reshape(channels, 8 * wide)
-    at += 8 * channels
-    grad_down = jnp.transpose(
-        sums[at : at + 4 * wide].reshape(2, 2, wide, 2, channels), (2, 0, 3, 1, 4)
-    ).reshape(wide, 8 * channels)
+    sums = sum_all(packed, chunk, counts, 3)
+    grad_first, grad_down, grad_coarse, grad_up, grad_last = call(
+        unpack_kernel,
+        [sums],
+        [
+            shape((channels, 27 * channels), F32),
+            shape((wide, 8 * channels), F32),
+            shape((wide, 27 * wide), F32),
+            shape((channels, 8 * wide), F32),
+            shape((channels, 27 * channels), F32),
+        ],
+        [],
+        "unpack",
+    )
     output = jnp.transpose(output.reshape(size_y, channels, size_x, size_z), (1, 2, 0, 3))
     return (output, grad_first, grad_down, grad_coarse, grad_up, grad_last)
 

time: 223 us -> 146 us (0.65)
  local copies, waits for them, and re-layouts: 79.3 us -> 8.51 us
  other arithmetic: 7.24 us -> 0 us
    reshape x17 -> x0, local copies, waits for them, and re-layouts: 44.8 us -> none  [the longest x7 35.5 us: banded(): jnp.stack(bands, axis=1)]
    another operation x8 -> x0, local copies, waits for them, and re-layouts: 14.1 us -> none  [banded(): jnp.stack(bands, axis=1)]
    transpose x12 -> x0, local copies, waits for them, and re-layouts: 6.65 us -> none  [the longest x2 2.91 us: fine_grad(): jnp.transpose(units, (2, 0, 3, 1, 4)).reshape(channels, 27 * channels)]
    another operation x5 -> x0, other arithmetic: 6.18 us -> none  [banded(): jnp.stack(bands, axis=1)]
    unnamed x38 -> x6, local copies, waits for them, and re-layouts: 6.98 us -> 1.79 us
    pad x0 -> x2, local copies, waits for them, and re-layouts: none -> 3.41 us  [shards(): whole = lambda v: jnp.pad(v, ((0, 0), (0, channels)))]
    slice x6 -> x0, local copies, waits for them, and re-layouts: 2.75 us -> none  [the longest x1 1.32 us: shards(): sums[at:at + 27 * wide].reshape(27, wide, wide)]
    pallas_call x7 -> x8, Pallas kernels: 133 us -> 135 us  [call(): pl.pallas_call(kernel, out_shape=outs, in_specs=[pl.BlockSpec(memory_spac...]
where the time goes in v1:
time: 146 us; the launch traced here: 144 us
  Pallas kernels  135 us (92%)
  local copies, waits for them, and re-layouts  8.51 us (6%)
    pallas_call x8, Pallas kernels, call(): pl.pallas_call(kernel, out_shape=outs, in_specs=[pl.BlockSpec(memory_spac...  135 us
    pad x2, local copies, waits for them, and re-layouts, shards(): whole = lambda v: jnp.pad(v, ((0, 0), (0, channels)))  3.41 us

profile of v1, /device:TPU:0, one launch (start us, length us, event | category | flops | bytes accessed | tf_op | source)
XLA Modules:
  0.0 144.2 jit_solution(13735326656303869561)
XLA Ops:
  0.6 0.0 copy-start
  0.6 1.7 %pad.8.weight_last = bf16[64,1792]{1,0:T(8,128)(2,1)} pad(bf16[64,1728]{1,0:T(8,128)(2,1)} %param.12, bf16[]{:T(256)} %constant.2.clone.1), padding=0_0x0_64 | pad | bytes 450562 | tf_op jit(solution)/shard_map/jit(_pad)/pad | solution.py:606
  2.3 0.0 copy-start.1
  2.3 1.7 %pad.7.weight_first = bf16[64,1792]{1,0:T(8,128)(2,1)} pad(bf16[64,1728]{1,0:T(8,128)(2,1)} %param.8, bf16[]{:T(256)} %constant.2.clone.1), padding=0_0x0_64 | pad | bytes 450562 | tf_op jit(solution)/shard_map/jit(_pad)/pad | solution.py:606
  4.1 0.0 copy-done
  4.1 0.2 copy.13
  4.3 0.9 copy.16
  5.2 0.0 copy-done.1
  5.2 0.2 copy.14
  5.4 0.9 copy.17
  6.3 15.6 %halo0.1 = (bf16[384,1536]{1,0:T(8,128)(2,1)}, bf16[384,1536]{1,0:T(8,128)(2,1)}) custom-call(bf16[256,1024]{1,0:T(8,128)(2,1)} %bitcast.11, bf16[256,1024]{1,0:T(8,128)(2,1)} %bitcast.12), custom_call_target="tpu_custom_call" | custom-call | tf_op jit(solution)/shard_map/halo0/pallas_call | solution.py:38
  21.8 12.4 %first.1 = (bf16[256,1024]{1,0:T(8,128)(2,1)}, bf16[256,256]{1,0:T(8,128)(2,1)}, f32[256,1024]{1,0:T(8,128)}, bf16[384,1536]{1,0:T(8,128)(2,1)}, bf16[256,1024]{1,0:T(8,128)(2,1)}) custom-call(bf16[384,1536]{1,0:T(8,128)(2,1)} %get-tuple-element.25.field, bf16[384,1536]{1,0:T(8,128)(2,1)} %get-tuple-element.26.cotan, bf16[64,1792]{1,0:T(8,128)(2,1)} %pad.7.weight_first, ...), custom_call_target="tpu_custom_call" | custom-call | tf_op jit(solution)/shard_map/first/pallas_call | solution.py:38
  34.2 15.8 %halo1.1.coarse = bf16[512,512]{1,0:T(8,128)(2,1)} custom-call(bf16[256,256]{1,0:T(8,128)(2,1)} %get-tuple-element.27.refs_0_), custom_call_target="tpu_custom_call" | custom-call | tf_op jit(solution)/shard_map/halo1/pallas_call | solution.py:38
  50.0 5.2 %level.1 = (bf16[256,1024]{1,0:T(8,128)(2,1)}, bf16[256,256]{1,0:T(8,128)(2,1)}, f32[512,128]{1,0:T(8,128)}) custom-call(bf16[512,512]{1,0:T(8,128)(2,1)} %halo1.1.coarse, bf16[128,3456]{1,0:T(8,128)(2,1)} %weight_coarse.3, bf16[64,1024]{1,0:T(8,128)(2,1)} %weight_up.1, bf16[256,1024]{1,0:T(8,128)(2,1)} %get-tuple-element.28.hidden, ...), custom_call_target="tpu_custom_call" | custom-call | tf_op jit(solution)/shard_map/level/pallas_call | solution.py:38
  55.2 13.9 %halo2.1 = (bf16[384,1536]{1,0:T(8,128)(2,1)}, bf16[512,512]{1,0:T(8,128)(2,1)}) custom-call(bf16[256,1024]{1,0:T(8,128)(2,1)} %get-tuple-element.30.refs_0_, bf16[256,256]{1,0:T(8,128)(2,1)} %get-tuple-element.31.refs_1_), custom_call_target="tpu_custom_call" | custom-call | tf_op jit(solution)/shard_map/halo2/pallas_call | solution.py:38
  69.1 18.1 %last.1 = (bf16[256,1024]{1,0:T(8,128)(2,1)}, bf16[6656,128]{1,0:T(8,128)(2,1)}) custom-call(bf16[384,1536]{1,0:T(8,128)(2,1)} %get-tuple-element.32.summed, bf16[512,512]{1,0:T(8,128)(2,1)} %get-tuple-element.33.back_level, bf16[512,512]{1,0:T(8,128)(2,1)} %halo1.1.coarse, bf16[256,1024]{1,0:T(8,128)(2,1)} %get-tuple-element.28.hidden, ...), custom_call_target="tpu_custom_call" | custom-call | tf_op jit(solution)/shard_map/last/pallas_call | solution.py:38
  87.2 1.4 reshape.23
  88.6 1.5 %copy.19 = bf16[4,64,4,256]{3,0,2,1:T(4,128)(2,1)} copy(bf16[4,64,4,256]{3,2,1,0:T(4,128)(2,1)S(1)} %reshape.23) | data formatting | bytes 1048576 | tf_op jit(solution)/shard_map/reshape | solution.py:685
  90.1 50.8 %sum_all.1.sums = bf16[6656,128]{1,0:T(8,128)(2,1)} custom-call(bf16[6656,128]{1,0:T(8,128)(2,1)} %get-tuple-element.38.x_ref), custom_call_target="tpu_custom_call" | custom-call | tf_op jit(solution)/shard_map/sum_all/pallas_call | solution.py:38
  140.9 3.3 %unpack.1 = (f32[64,1728]{1,0:T(8,128)}, f32[128,512]{1,0:T(8,128)}, f32[128,3456]{1,0:T(8,128)}, f32[64,1024]{1,0:T(8,128)}, f32[64,1728]{1,0:T(8,128)}) custom-call(bf16[6656,128]{1,0:T(8,128)(2,1)} %sum_all.1.sums), custom_call_target="tpu_custom_call" | custom-call | tf_op jit(solution)/shard_map/unpack/pallas_call | solution.py:38
Async XLA Ops:
  0.6 3.4 %copy-start = (bf16[64,4,4,256]{3,2,1,0:T(4,128)(2,1)S(1)}, bf16[64,4,4,256]{3,2,1,0:T(4,128)(2,1)}, u32[]{:S(2)}) copy-start(bf16[64,4,4,256]{3,2,1,0:T(4,128)(2,1)} %param.7) | copy-start | bytes 1572868
  2.3 2.8 %copy-start.1 = (bf16[64,4,4,256]{3,2,1,0:T(4,128)(2,1)S(1)}, bf16[64,4,4,256]{3,2,1,0:T(4,128)(2,1)}, u32[]{:S(2)}) copy-start(bf16[64,4,4,256]{3,2,1,0:T(4,128)(2,1)} %param.13) | copy-start | bytes 1572868

commit v2 on v1

--- a/solution.py
+++ b/solution.py
@@ -46,101 +46,90 @@
     )(*args)
 
 
-def halo_kernel(sizes, counts, *refs):
-    number = len(sizes)
-    ins, outs, (send, recv) = refs[:number], refs[number : 2 * number], refs[2 * number :]
-    n_x, n_y = counts
-    me_x, me_y = lax.axis_index("gx"), lax.axis_index("gy")
-    steps = [(i, j) for i in (-1, 0, 1) for j in (-1, 0, 1) if (i, j) != (0, 0)]
-
-    def inside(step_x, step_y):
-        at_x, at_y = me_x + step_x, me_y + step_y
-        return (at_x >= 0) & (at_x < n_x) & (at_y >= 0) & (at_y < n_y)
-
-    def place(step_x, step_y):
-        return (
-            jnp.clip(me_x + step_x, 0, n_x - 1),
-            jnp.clip(me_y + step_y, 0, n_y - 1),
+STEPS = [(i, j) for i in (-1, 0, 1) for j in (-1, 0, 1) if (i, j) != (0, 0)]
+
+
+def inside(counts, step):
+    at_x, at_y = lax.axis_index("gx") + step[0], lax.axis_index("gy") + step[1]
+    return (at_x >= 0) & (at_x < counts[0]) & (at_y >= 0) & (at_y < counts[1])
+
+
+def place(counts, step):
+    return (
+        jnp.clip(lax.axis_index("gx") + step[0], 0, counts[0] - 1),
+        jnp.clip(lax.axis_index("gy") + step[1], 0, counts[1] - 1),
+    )
+
+
+def greet(counts):
+    barrier = pltpu.get_barrier_semaphore()
+    for step in STEPS:
+
+        @pl.when(inside(counts, step))
+        def _(step=step):
+            pl.semaphore_signal(barrier, inc=1, device_id=place(counts, step), device_id_type=MESH)
+
+    pl.semaphore_wait(barrier, sum(inside(counts, step).astype(jnp.int32) for step in STEPS))
+
+
+def clear_rim(counts, wide, rim):
+    for step_x, step_y in STEPS:
+        spans = []
+        for step, extent, width in ((step_y, wide.shape[0], rim[0]), (step_x, wide.shape[1], rim[1])):
+            start = {-1: 0, 0: width, 1: extent - width}[step]
+            spans.append((start, extent - 2 * width if step == 0 else width))
+        (row, rows), (lane, lanes) = spans
+
+        @pl.when(jnp.logical_not(inside(counts, (step_x, step_y))))
+        def _(row=row, rows=rows, lane=lane, lanes=lanes):
+            wide[row : row + rows, lane : lane + lanes] = jnp.zeros((rows, lanes), BF16)
+
+
+def send_rim(counts, wide, rim, send, recv, which):
+    copies = []
+    for at, step in enumerate(STEPS):
+        source, target = [], []
+        for move, extent, width in ((step[1], wide.shape[0], rim[0]), (step[0], wide.shape[1], rim[1])):
+            if move == 0:
+                source.append(pl.ds(width, extent - 2 * width))
+                target.append(pl.ds(width, extent - 2 * width))
+            elif move > 0:
+                source.append(pl.ds(extent - 2 * width, width))
+                target.append(pl.ds(0, width))
+            else:
+                source.append(pl.ds(width, width))
+                target.append(pl.ds(extent - width, width))
+        copy = pltpu.make_async_remote_copy(
+            src_ref=wide.at[tuple(source)],
+            dst_ref=wide.at[tuple(target)],
+            send_sem=send.at[which, at],
+            recv_sem=recv.at[which, at],
+            device_id=place(counts, step),
+            device_id_type=MESH,
         )
-
-    barrier = pltpu.get_barrier_semaphore()
-    for step in steps:
-
-        @pl.when(inside(*step))
-        def _(step=step):
-            pl.semaphore_signal(barrier, inc=1, device_id=place(*step), device_id_type=MESH)
-
-    pl.semaphore_wait(barrier, sum(inside(*step).astype(jnp.int32) for step in steps))
-
-    def spans(step, extent, width):
-        if step == 0:
-            return pl.ds(0, extent), pl.ds(width, extent)
-        if step > 0:
-            return pl.ds(extent - width, width), pl.ds(0, width)
-        return pl.ds(0, width), pl.ds(width + extent, width)
-
-    copies = []
-    for at, (step_x, step_y) in enumerate(steps):
-        for which, (row_width, lane_width) in enumerate(sizes):
-            rows, lanes = ins[which].shape
-            row_from, row_to = spans(step_y, rows, row_width)
-            lane_from, lane_to = spans(step_x, lanes, lane_width)
-            copies.append(
-                (
-                    step_x,
-                    step_y,
-                    pltpu.make_async_remote_copy(
-                        src_ref=ins[which].at[row_from, lane_from],
-                        dst_ref=outs[which].at[row_to, lane_to],
-                        send_sem=send.at[at, which],
-                        recv_sem=recv.at[at, which],
-                        device_id=place(step_x, step_y),
-                        device_id_type=MESH,
-                    ),
-                )
-            )
-    for step_x, step_y, copy in copies:
-
-        @pl.when(inside(step_x, step_y))
+        copies.append((step, copy))
+
+        @pl.when(inside(counts, step))
         def _(copy=copy):
             copy.start()
 
-    for which, (row_width, lane_width) in enumerate(sizes):
-        rows, lanes = ins[which].shape
-        outs[which][row_width : row_width + rows, lane_width : lane_width + lanes] = ins[which][...]
-        for step_x, step_y in steps:
-            row_at = {-1: (0, row_width), 0: (row_width, rows), 1: (row_width + rows, row_width)}[step_y]
-            lane_at = {-1: (0, lane_width), 0: (lane_width, lanes), 1: (lane_width + lanes, lane_width)}[step_x]
-
-            @pl.when(jnp.logical_not(inside(step_x, step_y)))
-            def _(row_at=row_at, lane_at=lane_at, which=which):
-                outs[which][
-                    row_at[0] : row_at[0] + row_at[1], lane_at[0] : lane_at[0] + lane_at[1]
-                ] = jnp.zeros((row_at[1], lane_at[1]), BF16)
-
-    for step_x, step_y, copy in copies:
-
-        @pl.when(inside(-step_x, -step_y))
+    return copies
+
+
+def rim_arrived(counts, copies):
+    for step, copy in copies:
+
+        @pl.when(inside(counts, (-step[0], -step[1])))
         def _(copy=copy):
             copy.wait_recv()
 
-    for step_x, step_y, copy in copies:
-
-        @pl.when(inside(step_x, step_y))
+
+def rim_left(counts, copies):
+    for step, copy in copies:
+
+        @pl.when(inside(counts, step))
         def _(copy=copy):
             copy.wait_send()
-
-
-def halo(blocks, sizes, counts, collective):
-    outs = [
-        jax.ShapeDtypeStruct((b.shape[0] + 2 * r, b.shape[1] + 2 * l), b.dtype)
-        for b, (r, l) in zip(blocks, sizes)
-    ]
-    scratch = [pltpu.SemaphoreType.DMA((8, len(sizes))), pltpu.SemaphoreType.DMA((8, len(sizes)))]
-    return call(
-        functools.partial(halo_kernel, sizes, counts),
-        blocks, outs, scratch, "halo%d" % collective, collective,
-    )
 
 
 def sum_kernel(chunk, counts, x_ref, full, r1, s1, r2, s2, r3, send, recv):
@@ -417,92 +406,94 @@
     return jnp.concatenate(pieces, axis=0)
 
 
-def first_kernel(field, cotan, weight_first, weight_last, weight_down, hidden, coarse, back_sum, field_z, cotan_z, work, cells_ref, shifted, w_first, w_last_t, twice):
+def block_kernel(
+    counts, field, cotan, weight_first, weight_last, weight_down, weight_coarse, weight_up,
+    output, packed,
+    field_w, cotan_w, summed_w, coarse_w, level_w, hidden, back_sum, back_first,
+    shifted, shifted_c, w_first, w_last_t, w_last, w_coarse, w_coarse_t, twice,
+    cells_ref, cells_f32, total_ref, send, recv,
+):
     size = 2 * LANES
-    n_y = hidden.shape[0] // weight_first.shape[0]
+    channels = weight_first.shape[0]
+    rows, lanes = field.shape
+    n_x, n_y = lanes // size, rows // channels
+    n_qx, n_qy = n_x // 2, n_y // 2
+    width = n_qx * LANES
+    fine_rows, coarse_rows = field_w.shape[0], coarse_w.shape[0]
+    fine_rim, coarse_rim = (channels, size), (LANES, LANES)
+    left = left_half((channels, LANES))
+    n_cells = n_qx * n_qy * LANES
+
+    for wide in (field_w, cotan_w, summed_w):
+        clear_rim(counts, wide, fine_rim)
+    for wide in (coarse_w, level_w):
+        clear_rim(counts, wide, coarse_rim)
+    matrix = parity_matrix(size, False)
+    for source, wide in ((field, field_w), (cotan, cotan_w)):
+        for x in range(n_x):
+            wide[channels : channels + rows, (x + 1) * size : (x + 2) * size] = dot(
+                source[:, x * size : (x + 1) * size], matrix
+            ).astype(BF16)
+    greet(counts)
+    copies = [send_rim(counts, field_w, fine_rim, send, recv, 0)]
+    copies.append(send_rim(counts, cotan_w, fine_rim, send, recv, 1))
+
     band_fine(weight_first, twice, w_first, n_y, False)
     band_fine(weight_last, twice, w_last_t, n_y, True)
-    w_down = down_weight(weight_down).astype(BF16)
-    matrix = parity_matrix(size, False)
-    blocks = field.shape[1] // size
-    for x in range(blocks):
-        field_z[:, x * size : (x + 1) * size] = dot(field[:, x * size : (x + 1) * size], matrix).astype(BF16)
-        work[:, x * size : (x + 1) * size] = dot(cotan[:, x * size : (x + 1) * size], matrix).astype(BF16)
-    fine_shifts(field_z, shifted)
+    band_coarse(weight_coarse, w_coarse, n_qy, False)
+    w_down = down_weight(weight_down)
+    w_down_t = w_down.T.astype(BF16)
+    w_down = w_down.astype(BF16)
+    w_up = up_weight(weight_up)
+    w_up_t = w_up.T.astype(BF16)
+    w_up = w_up.astype(BF16)
+
+    rim_arrived(counts, copies[0])
+    fine_shifts(field_w, shifted)
 
     def store_hidden(where, value):
         hidden[:, where] = leaky(value).astype(BF16)
 
     fine_conv(shifted, w_first, store_hidden)
-    n_qx, n_qy = (blocks - 2) // 2, hidden.shape[0] // LANES
     for row, lane, fine_row, fine_lane in cells(n_qx, n_qy):
         cells_ref[part(row, lane)] = hidden[part(fine_row, fine_lane)]
     value = leaky(dot(w_down, cells_ref[...])).astype(BF16)
-    width = n_qx * LANES
     for qy in range(n_qy):
-        coarse[qy * LANES : (qy + 1) * LANES, :] = value[:, qy * width : (qy + 1) * width]
-    rim = (work.shape[0] - hidden.shape[0]) // 2
-    cotan_z[...] = work[rim : rim + hidden.shape[0], size : size + hidden.shape[1]]
-    fine_shifts(work, shifted)
+        coarse_w[(qy + 1) * LANES : (qy + 2) * LANES, LANES : LANES + width] = value[:, qy * width : (qy + 1) * width]
+    copies.append(send_rim(counts, coarse_w, coarse_rim, send, recv, 2))
+
+    rim_arrived(counts, copies[1])
+    fine_shifts(cotan_w, shifted)
 
     def store_back(where, value):
         back_sum[:, where] = value
 
     fine_conv(shifted, w_last_t, store_back)
 
-
-def level_kernel(coarse, weight_coarse, weight_up, hidden, back_sum, summed, back_level, grad_up, raised, back_cells, shifted, w_coarse):
-    coarse_shifts(coarse, shifted)
-    n_qx, n_qy = coarse.shape[1] // LANES - 2, coarse.shape[0] // LANES - 2
-    band_coarse(weight_coarse, w_coarse, n_qy, False)
-    w_up = up_weight(weight_up)
-    w_up_t = w_up.T.astype(BF16)
-    w_up = w_up.astype(BF16)
-    level = to_wide(leaky(coarse_conv(shifted, w_coarse)).astype(BF16), n_qy, LANES)
-    raised[...] = dot(w_up, level)
+    rim_arrived(counts, copies[2])
+    coarse_shifts(coarse_w, shifted_c)
+    level = to_wide(leaky(coarse_conv(shifted_c, w_coarse)).astype(BF16), n_qy, LANES)
+    cells_f32[...] = dot(w_up, level)
     for row, lane, fine_row, fine_lane in cells(n_qx, n_qy):
         here, fine = part(row, lane), part(fine_row, fine_lane)
-        value = raised[here]
+        value = cells_f32[here]
         root = lax.rsqrt(value * value + 1.0)
-        summed[fine] = (leaky(value) + hidden[fine].astype(F32)).astype(BF16)
-        back_cells[here] = (back_sum[fine] * (0.505 + 0.495 * value * root)).astype(BF16)
-    grad_up[...] = dot_nt(back_cells[...], level)
-    back = (dot(w_up_t, back_cells[...]) * slope_of(level)).astype(BF16)
-    width = n_qx * LANES
+        summed_w[
+            channels + fine_row * LANES : channels + (fine_row + 1) * LANES,
+            size + fine_lane * LANES : size + (fine_lane + 1) * LANES,
+        ] = (leaky(value) + hidden[fine].astype(F32)).astype(BF16)
+        cells_ref[here] = (back_sum[fine] * (0.505 + 0.495 * value * root)).astype(BF16)
+    back = (dot(w_up_t, cells_ref[...]) * slope_of(level)).astype(BF16)
     for qy in range(n_qy):
-        back_level[qy * LANES : (qy + 1) * LANES, :] = back[:, qy * width : (qy + 1) * width]
-
-
-def last_kernel(summed, back_level, coarse, hidden, back_sum, field_z, cotan_z, grad_up, weight_last, weight_coarse, weight_down, output, packed, shifted, shifted_c, back_first, cells_ref, spread, total_ref, w_last, w_coarse_t, twice):
-    size = 2 * LANES
-    matrix = parity_matrix(size, True)
+        level_w[(qy + 1) * LANES : (qy + 2) * LANES, LANES : LANES + width] = back[:, qy * width : (qy + 1) * width]
+    copies.append(send_rim(counts, level_w, coarse_rim, send, recv, 3))
+    copies.append(send_rim(counts, summed_w, fine_rim, send, recv, 4))
+
     packed[...] = jnp.zeros(packed.shape, BF16)
-    channels = 64
-    n_y = hidden.shape[0] // channels
-    n_qx, n_qy = coarse.shape[1] // LANES - 2, coarse.shape[0] // LANES - 2
-    width = n_qx * LANES
-    fine_rows = summed.shape[0]
-    coarse_rows = coarse.shape[0]
-    lanes = hidden.shape[1]
-    in_half = left_half((channels, LANES))
-    band_fine(weight_last, twice, w_last, n_y, False)
-    band_coarse(weight_coarse, w_coarse_t, n_qy, True)
-    w_down_t = down_weight(weight_down).T.astype(BF16)
-
-    coarse_shifts(back_level, shifted_c)
-    center = coarse[LANES : LANES * (1 + n_qy), LANES : LANES + width]
-    back = (coarse_conv(shifted_c, w_coarse_t) * slope_of(center)).astype(BF16)
-    back_wide = to_wide(back, n_qy, LANES)
-    spread[...] = dot(w_down_t, back_wide)
-    for row, lane, fine_row, fine_lane in cells(n_qx, n_qy):
-        here, fine = part(row, lane), part(fine_row, fine_lane)
-        mine = hidden[fine]
-        cells_ref[here] = mine
-        back_first[fine] = ((back_sum[fine] + spread[here]) * slope_of(mine)).astype(BF16)
-
+    base = 27 * channels + 27 * LANES
+    packed[base : base + 8 * channels, :] = dot_nt(cells_ref[...], level).astype(BF16)
     base = 27 * channels
-    coarse_shifts(coarse, shifted_c)
-    center = back_level[LANES : LANES * (1 + n_qy), LANES : LANES + width]
+    center = level_w[LANES : LANES * (1 + n_qy), LANES : LANES + width]
     for along_x in range(3):
         total_ref[:, : 3 * coarse_rows] = dot_nt(center, shifted_c[:, along_x * LANES : along_x * LANES + width])
         for along_z in range(3):
@@ -514,17 +505,28 @@
                     term = here if term is None else term + here
                 at = base + (along_x * 9 + along_y * 3 + along_z) * LANES
                 packed[at : at + LANES, :] = term.astype(BF16)
-    base = base + 27 * LANES
-    for k in range(8):
-        packed[base + k * 64 : base + k * 64 + 64, :] = grad_up[k * 64 : k * 64 + 64, :].astype(BF16)
-    base = base + 512
-    down = dot_nt(back_wide, cells_ref[...])
+    band_coarse(weight_coarse, w_coarse_t, n_qy, True)
+    band_fine(weight_last, twice, w_last, n_y, False)
+    fine_shifts(field_w, shifted)
+
+    rim_arrived(counts, copies[3])
+    coarse_shifts(level_w, shifted_c)
+    center = coarse_w[LANES : LANES * (1 + n_qy), LANES : LANES + width]
+    back = to_wide((coarse_conv(shifted_c, w_coarse_t) * slope_of(center)).astype(BF16), n_qy, LANES)
+    cells_f32[...] = dot(w_down_t, back)
+    for row, lane, fine_row, fine_lane in cells(n_qx, n_qy):
+        here, fine = part(row, lane), part(fine_row, fine_lane)
+        mine = hidden[fine]
+        cells_ref[here] = mine
+        back_first[fine] = ((back_sum[fine] + cells_f32[here]) * slope_of(mine)).astype(BF16)
+    base = 27 * channels + 27 * LANES + 8 * channels
+    down = dot_nt(back, cells_ref[...])
     for k in range(4):
         packed[base + k * LANES : base + (k + 1) * LANES, :] = down[:, k * LANES : (k + 1) * LANES].astype(BF16)
 
-    def weight_grad(left, second):
+    def weight_grad(value, second):
         for along_x in range(3):
-            total_ref[:, : 3 * fine_rows] = dot_nt(left[...], shifted[:, along_x * size : along_x * size + lanes])
+            total_ref[:, : 3 * fine_rows] = dot_nt(value, shifted[:, along_x * size : along_x * size + lanes])
             for along_z in range(3):
                 total = None
                 for y in range(n_y):
@@ -541,21 +543,24 @@
                     packed[at + channels : at + 2 * channels, :] = head
                     rest = pltpu.roll(rest, channels, 1)
                     packed[tail : tail + channels, :] = jnp.where(
-                        in_half, packed[tail : tail + channels, :].astype(F32), rest
+                        left, packed[tail : tail + channels, :].astype(F32), rest
                     ).astype(BF16)
                 else:
                     packed[at : at + channels, :] = head
                     packed[tail : tail + channels, :] = rest.astype(BF16)
 
-    fine_shifts(field_z, shifted)
-    weight_grad(back_first, False)
-    fine_shifts(summed, shifted)
-    weight_grad(cotan_z, True)
+    weight_grad(back_first[...], False)
+    rim_arrived(counts, copies[4])
+    fine_shifts(summed_w, shifted)
+    weight_grad(cotan_w[channels : channels + rows, size : size + lanes], True)
+    matrix = parity_matrix(size, True)
 
     def store(where, value):
         output[:, where] = dot(value.astype(BF16), matrix).astype(BF16)
 
     fine_conv(shifted, w_last, store)
+    for group in copies:
+        rim_left(counts, group)
 
 
 def unpack_kernel(sums, first, down, coarse, up, last):
@@ -605,68 +610,37 @@
 
     whole = lambda v: jnp.pad(v, ((0, 0), (0, channels)))
     weight_first, weight_last = whole(weight_first), whole(weight_last)
-    fine_rim, coarse_rim = (channels, size_z), (wide, size_z // 2)
-    field_w, cotan_w = halo([fine(field), fine(cotangent)], [fine_rim, fine_rim], counts, 0)
-    full_rows, full_lanes = field_w.shape
+    wide_rows, wide_lanes = (size_y + 2) * channels, (size_x + 2) * size_z
+    coarse_rows, coarse_lanes = (n_qy + 2) * wide, (n_qx + 2) * LANES
     n_cells = n_qx * n_qy * LANES
-    hidden, coarse, back_sum, field_z, cotan_z = call(
-        first_kernel,
-        [field_w, cotan_w, weight_first, weight_last, weight_down],
-        [
-            shape((rows, lanes), BF16),
-            shape((n_qy * wide, n_qx * LANES), BF16),
-            shape((rows, lanes), F32),
-            shape((full_rows, full_lanes), BF16),
-            shape((rows, lanes), BF16),
-        ],
-        [
-            pltpu.VMEM((full_rows, full_lanes), BF16),
-            pltpu.VMEM((8 * channels, n_cells), BF16),
-            pltpu.VMEM((3 * full_rows, full_lanes), BF16),
-            pltpu.VMEM((3, rows, 3 * full_rows), BF16),
-            pltpu.VMEM((3, rows, 3 * full_rows), BF16),
-            pltpu.VMEM((27 * channels, LANES), F32),
-        ],
-        "first",
-    )
-    (coarse_w,) = halo([coarse], [coarse_rim], counts, 1)
-    coarse_rows, coarse_lanes = coarse_w.shape
-    summed, back_level, grad_up = call(
-        level_kernel,
-        [coarse_w, weight_coarse, weight_up, hidden, back_sum],
-        [
-            shape((rows, lanes), BF16),
-            shape((n_qy * wide, n_qx * LANES), BF16),
-            shape((8 * channels, wide), F32),
-        ],
-        [
-            pltpu.VMEM((8 * channels, n_cells), F32),
-            pltpu.VMEM((8 * channels, n_cells), BF16),
-            pltpu.VMEM((3 * coarse_rows, coarse_lanes), BF16),
-            pltpu.VMEM((3, n_qy * wide, 3 * coarse_rows), BF16),
-        ],
-        "level",
-    )
-    summed_w, back_level_w = halo([summed, back_level], [fine_rim, coarse_rim], counts, 2)
     used = 27 * channels + 27 * wide + 8 * channels + 4 * wide
     devices = counts[0] * counts[1]
     chunk = -(-used // (devices * 16)) * 16
     output, packed = call(
-        last_kernel,
-        [summed_w, back_level_w, coarse_w, hidden, back_sum, field_z, cotan_z, grad_up, weight_last, weight_coarse, weight_down],
+        functools.partial(block_kernel, counts),
+        [fine(field), fine(cotangent), weight_first, weight_last, weight_down, weight_coarse, weight_up],
         [shape((rows, lanes), BF16), shape((chunk * devices, LANES), BF16)],
-        [
-            pltpu.VMEM((3 * full_rows, full_lanes), BF16),
+        [pltpu.VMEM((wide_rows, wide_lanes), BF16)] * 3
+        + [pltpu.VMEM((coarse_rows, coarse_lanes), BF16)] * 2
+        + [
+            pltpu.VMEM((rows, lanes), BF16),
+            pltpu.VMEM((rows, lanes), F32),
+            pltpu.VMEM((rows, lanes), BF16),
+            pltpu.VMEM((3 * wide_rows, wide_lanes), BF16),
             pltpu.VMEM((3 * coarse_rows, coarse_lanes), BF16),
-            pltpu.VMEM((rows, lanes), BF16),
+        ]
+        + [pltpu.VMEM((3, rows, 3 * wide_rows), BF16)] * 3
+        + [pltpu.VMEM((3, n_qy * wide, 3 * coarse_rows), BF16)] * 2
+        + [
+            pltpu.VMEM((27 * channels, LANES), F32),
             pltpu.VMEM((8 * channels, n_cells), BF16),
             pltpu.VMEM((8 * channels, n_cells), F32),
-            pltpu.VMEM((max(rows, n_qy * wide), 3 * max(full_rows, coarse_rows)), F32),
-            pltpu.VMEM((3, rows, 3 * full_rows), BF16),
-            pltpu.VMEM((3, n_qy * wide, 3 * coarse_rows), BF16),
-            pltpu.VMEM((27 * channels, LANES), F32),
+            pltpu.VMEM((max(rows, n_qy * wide), 3 * max(wide_rows, coarse_rows)), F32),
+            pltpu.SemaphoreType.DMA((5, 8)),
+            pltpu.SemaphoreType.DMA((5, 8)),
         ],
-        "last",
+        "block",
+        0,
     )
     sums = sum_all(packed, chunk, counts, 3)
     grad_first, grad_down, grad_coarse, grad_up, grad_last = call(

time: 146 us -> 110 us (0.75)
  Pallas kernels: 135 us -> 99.1 us
    pallas_call x8 -> x3, Pallas kernels: 135 us -> 99.1 us  [call(): pl.pallas_call(kernel, out_shape=outs, in_specs=[pl.BlockSpec(memory_spac...]
where the time goes in v2:
time: 110 us; the launch traced here: 109 us
  Pallas kernels  99.1 us (90%)
  local copies, waits for them, and re-layouts  9.49 us (9%)
    pallas_call x3, Pallas kernels, call(): pl.pallas_call(kernel, out_shape=outs, in_specs=[pl.BlockSpec(memory_spac...  99.1 us
    pad x2, local copies, waits for them, and re-layouts, shards(): whole = lambda v: jnp.pad(v, ((0, 0), (0, channels)))  3.35 us
    reshape x2, local copies, waits for them, and re-layouts, shards(): output.reshape(size_y, channels, size_x, size_z)  2.91 us

profile of v2, /device:TPU:0, one launch (start us, length us, event | category | flops | bytes accessed | tf_op | source)
XLA Modules:
  0.0 109.3 jit_solution(4601195431948418890)
XLA Ops:
  0.6 0.0 copy-start
  0.6 1.7 %pad.7.weight_first = bf16[64,1792]{1,0:T(8,128)(2,1)} pad(bf16[64,1728]{1,0:T(8,128)(2,1)} %param.8, bf16[]{:T(256)} %constant.2.clone.1), padding=0_0x0_64 | pad | bytes 450562 | tf_op jit(solution)/shard_map/jit(_pad)/pad | solution.py:611
  2.3 1.6 %pad.8.weight_last = bf16[64,1792]{1,0:T(8,128)(2,1)} pad(bf16[64,1728]{1,0:T(8,128)(2,1)} %param.12, bf16[]{:T(256)} %constant.2.clone.1), padding=0_0x0_64 | pad | bytes 450562 | tf_op jit(solution)/shard_map/jit(_pad)/pad | solution.py:611
  4.0 1.2 %copy.13 = bf16[4,64,4,256]{3,2,1,0:T(4,128)(2,1)S(1)} copy(bf16[4,64,4,256]{3,0,2,1:T(4,128)(2,1)} %bitcast.15) | data formatting | bytes 1048576 | tf_op jit(solution)/shard_map/transpose | solution.py:608
  5.2 0.9 copy.16
  6.1 0.0 copy-done
  6.1 0.2 copy.14
  6.3 0.9 copy.17
  7.2 48.2 %block.1 = (bf16[256,1024]{1,0:T(8,128)(2,1)}, bf16[6656,128]{1,0:T(8,128)(2,1)}) custom-call(bf16[256,1024]{1,0:T(8,128)(2,1)} %bitcast.13, bf16[256,1024]{1,0:T(8,128)(2,1)} %bitcast.14, bf16[64,1792]{1,0:T(8,128)(2,1)} %pad.7.weight_first, bf16[64,1792]{1,0:T(8,128)(2,1)} %pad.8.weight_last, bf16[128,512]{1,0:T(8,128)(2,1)} %weight_down.1, ...), custom_call_target="tpu_custom_call" | custom-call | tf_op jit(solution)/shard_map/block/pallas_call | solution.py:38
  55.4 1.4 %reshape.23 = bf16[4,64,4,256]{3,2,1,0:T(4,128)(2,1)S(1)} reshape(bf16[256,1024]{1,0:T(8,128)(2,1)} %get-tuple-element.13) | data formatting | bytes 1048576 | tf_op jit(solution)/shard_map/reshape | solution.py:659
  56.9 1.5 %copy.19 = bf16[4,64,4,256]{3,0,2,1:T(4,128)(2,1)} copy(bf16[4,64,4,256]{3,2,1,0:T(4,128)(2,1)S(1)} %reshape.23) | data formatting | bytes 1048576 | tf_op jit(solution)/shard_map/reshape | solution.py:659
  58.3 47.6 %sum_all.1.sums = bf16[6656,128]{1,0:T(8,128)(2,1)} custom-call(bf16[6656,128]{1,0:T(8,128)(2,1)} %get-tuple-element.14.x_ref), custom_call_target="tpu_custom_call" | custom-call | tf_op jit(solution)/shard_map/sum_all/pallas_call | solution.py:38
  106.0 3.3 %unpack.1 = (f32[64,1728]{1,0:T(8,128)}, f32[128,512]{1,0:T(8,128)}, f32[128,3456]{1,0:T(8,128)}, f32[64,1024]{1,0:T(8,128)}, f32[64,1728]{1,0:T(8,128)}) custom-call(bf16[6656,128]{1,0:T(8,128)(2,1)} %sum_all.1.sums), custom_call_target="tpu_custom_call" | custom-call | tf_op jit(solution)/shard_map/unpack/pallas_call | solution.py:38
Async XLA Ops:
  0.6 5.5 %copy-start = (bf16[64,4,4,256]{3,2,1,0:T(4,128)(2,1)S(1)}, bf16[64,4,4,256]{3,2,1,0:T(4,128)(2,1)}, u32[]{:S(2)}) copy-start(bf16[64,4,4,256]{3,2,1,0:T(4,128)(2,1)} %param.13) | copy-start | bytes 1572868

commit v3 on v2

--- a/solution.py
+++ b/solution.py
@@ -132,7 +132,40 @@
             copy.wait_send()
 
 
-def sum_kernel(chunk, counts, x_ref, full, r1, s1, r2, s2, r3, send, recv):
+def sum_kernel(chunks, counts, x_ref, full, *refs):
+    send, recv = refs[-2:]
+    streams, start = [], 0
+    greet_sum(counts)
+    for k, chunk in enumerate(chunks):
+        size = chunk * counts[0] * counts[1]
+        part_of = pl.ds(start, size)
+        streams.append(
+            sum_stream(
+                chunk, counts, x_ref.at[part_of], full.at[part_of],
+                *refs[5 * k : 5 * k + 5], send.at[k], recv.at[k],
+            )
+        )
+        start += size
+    ended = object()
+    while streams:
+        streams = [stream for stream in streams if next(stream, ended) is not ended]
+
+
+def greet_sum(counts):
+    n_x, n_y = counts
+    n_z = n_x // 2
+    me_x, me_y = lax.axis_index("gx"), lax.axis_index("gy")
+    core, me_z = lax.rem(me_x, 2), me_x // 2
+    peers = [(me_z * 2 + 1 - core, me_y)]
+    peers += [(me_x, lax.rem(me_y + k, n_y)) for k in range(1, n_y)]
+    peers += [(lax.rem(me_z + k, n_z) * 2 + core, me_y) for k in range(1, n_z)]
+    barrier = pltpu.get_barrier_semaphore()
+    for peer in peers:
+        pl.semaphore_signal(barrier, inc=1, device_id=peer, device_id_type=MESH)
+    pl.semaphore_wait(barrier, len(peers))
+
+
+def sum_stream(chunk, counts, x_ref, full, r1, s1, r2, s2, r3, send, recv):
     n_x, n_y = counts
     n_z = n_x // 2
     me_x, me_y = lax.axis_index("gx"), lax.axis_index("gy")
@@ -151,12 +184,6 @@
 
     def z_place(step):
         return (z_peer(step) * 2 + core, me_y)
-
-    barrier = pltpu.get_barrier_semaphore()
-    peers = [twin] + [y_place(k) for k in range(1, n_y)] + [z_place(k) for k in range(1, n_z)]
-    for peer in peers:
-        pl.semaphore_signal(barrier, inc=1, device_id=peer, device_id_type=MESH)
-    pl.semaphore_wait(barrier, len(peers))
 
     def copy(src, dst, at, place):
         made = pltpu.make_async_remote_copy(
@@ -173,6 +200,7 @@
     count = 0
     mine = core * half
     one = copy(x_ref.at[rows((1 - core) * half, half)], r1, 0, twin)
+    yield
     one.wait_recv()
     started.append(one)
     s1[...] = (x_ref[rows(mine, half), :].astype(F32) + r1[...].astype(F32)).astype(BF16)
@@ -181,6 +209,7 @@
     for k in range(1, n_y):
         group.append(copy(s1.at[rows(y_peer(k) * mid, mid)], r2.at[k - 1], count, y_place(k)))
         count += 1
+    yield
     total = s1[rows(me_y * mid, mid), :].astype(F32)
     for k, made in enumerate(group):
         made.wait_recv()
@@ -191,6 +220,7 @@
     for k in range(1, n_z):
         group.append(copy(s2.at[rows(z_peer(k) * chunk, chunk)], r3.at[k - 1], count, z_place(k)))
         count += 1
+    yield
     total = s2[rows(me_z * chunk, chunk), :].astype(F32)
     for k, made in enumerate(group):
         made.wait_recv()
@@ -203,6 +233,7 @@
     for k in range(1, n_z):
         group.append(copy(full.at[own], full.at[own], count, z_place(k)))
         count += 1
+    yield
     for made in group:
         made.wait_recv()
     started += group
@@ -211,33 +242,36 @@
     for k in range(1, n_y):
         group.append(copy(full.at[own], full.at[own], count, y_place(k)))
         count += 1
+    yield
     for made in group:
         made.wait_recv()
     started += group
     own = rows(mine, half)
     last = copy(full.at[own], full.at[own], count, twin)
+    yield
     last.wait_recv()
     started.append(last)
     for made in started:
         made.wait_send()
 
 
-def sum_all(packed, chunk, counts, collective):
+def sum_all(packed, chunks, counts, collective):
     n_x, n_y = counts
     n_z = n_x // 2
     copies = 2 + 2 * (n_y - 1) + 2 * (n_z - 1)
-    half, mid = chunk * n_z * n_y, chunk * n_z
-    scratch = [
-        pltpu.VMEM((half, LANES), BF16),
-        pltpu.VMEM((half, LANES), BF16),
-        pltpu.VMEM((max(n_y - 1, 1), mid, LANES), BF16),
-        pltpu.VMEM((mid, LANES), BF16),
-        pltpu.VMEM((max(n_z - 1, 1), chunk, LANES), BF16),
-        pltpu.SemaphoreType.DMA((copies,)),
-        pltpu.SemaphoreType.DMA((copies,)),
-    ]
+    scratch = []
+    for chunk in chunks:
+        half, mid = chunk * n_z * n_y, chunk * n_z
+        scratch += [
+            pltpu.VMEM((half, LANES), BF16),
+            pltpu.VMEM((half, LANES), BF16),
+            pltpu.VMEM((max(n_y - 1, 1), mid, LANES), BF16),
+            pltpu.VMEM((mid, LANES), BF16),
+            pltpu.VMEM((max(n_z - 1, 1), chunk, LANES), BF16),
+        ]
+    scratch += [pltpu.SemaphoreType.DMA((len(chunks), copies))] * 2
     return call(
-        functools.partial(sum_kernel, chunk, counts),
+        functools.partial(sum_kernel, chunks, counts),
         [packed], [jax.ShapeDtypeStruct(packed.shape, BF16)], scratch, "sum_all", collective,
     )[0]
 
@@ -642,7 +676,9 @@
         "block",
         0,
     )
-    sums = sum_all(packed, chunk, counts, 3)
+    first_part = -(-chunk // 32) * 16
+    chunks = [size for size in (first_part, chunk - first_part) if size > 0]
+    sums = sum_all(packed, chunks, counts, 3)
     grad_first, grad_down, grad_coarse, grad_up, grad_last = call(
         unpack_kernel,
         [sums],

time: 110 us -> 105 us (0.955)
  Pallas kernels: 99.1 us -> 94.4 us
    pallas_call x3, Pallas kernels: 99.1 us -> 94.4 us  [call(): pl.pallas_call(kernel, out_shape=outs, in_specs=[pl.BlockSpec(memory_spac...]
where the time goes in v3:
time: 105 us
  Pallas kernels  94.4 us (90%)
  local copies, waits for them, and re-layouts  9.49 us (9%)
    pallas_call x3, Pallas kernels, call(): pl.pallas_call(kernel, out_shape=outs, in_specs=[pl.BlockSpec(memory_spac...  94.4 us
    pad x2, local copies, waits for them, and re-layouts, shards(): whole = lambda v: jnp.pad(v, ((0, 0), (0, channels)))  3.35 us
    reshape x2, local copies, waits for them, and re-layouts, shards(): output.reshape(size_y, channels, size_x, size_z)  2.91 us

profile of v3, /device:TPU:0, one launch (start us, length us, event | category | flops | bytes accessed | tf_op | source)
XLA Modules:
  0.0 104.6 jit_solution(11923643607638714455)
XLA Ops:
  0.6 0.0 copy-start
  0.6 1.7 %pad.7.weight_first = bf16[64,1792]{1,0:T(8,128)(2,1)} pad(bf16[64,1728]{1,0:T(8,128)(2,1)} %param.8, bf16[]{:T(256)} %constant.2.clone.1), padding=0_0x0_64 | pad | bytes 450562 | tf_op jit(solution)/shard_map/jit(_pad)/pad | solution.py:645
  2.3 1.6 %pad.8.weight_last = bf16[64,1792]{1,0:T(8,128)(2,1)} pad(bf16[64,1728]{1,0:T(8,128)(2,1)} %param.12, bf16[]{:T(256)} %constant.2.clone.1), padding=0_0x0_64 | pad | bytes 450562 | tf_op jit(solution)/shard_map/jit(_pad)/pad | solution.py:645
  4.0 1.2 %copy.13 = bf16[4,64,4,256]{3,2,1,0:T(4,128)(2,1)S(1)} copy(bf16[4,64,4,256]{3,0,2,1:T(4,128)(2,1)} %bitcast.15) | data formatting | bytes 1048576 | tf_op jit(solution)/shard_map/transpose | solution.py:642
  5.2 0.9 copy.16
  6.1 0.0 copy-done
  6.1 0.2 copy.14
  6.3 0.9 copy.17
  7.2 48.2 %block.1 = (bf16[256,1024]{1,0:T(8,128)(2,1)}, bf16[6656,128]{1,0:T(8,128)(2,1)}) custom-call(bf16[256,1024]{1,0:T(8,128)(2,1)} %bitcast.13, bf16[256,1024]{1,0:T(8,128)(2,1)} %bitcast.14, bf16[64,1792]{1,0:T(8,128)(2,1)} %pad.7.weight_first, bf16[64,1792]{1,0:T(8,128)(2,1)} %pad.8.weight_last, bf16[128,512]{1,0:T(8,128)(2,1)} %weight_down.1, ...), custom_call_target="tpu_custom_call" | custom-call | tf_op jit(solution)/shard_map/block/pallas_call | solution.py:38
  55.4 1.4 %reshape.23 = bf16[4,64,4,256]{3,2,1,0:T(4,128)(2,1)S(1)} reshape(bf16[256,1024]{1,0:T(8,128)(2,1)} %get-tuple-element.13) | data formatting | bytes 1048576 | tf_op jit(solution)/shard_map/reshape | solution.py:695
  56.9 1.5 %copy.19 = bf16[4,64,4,256]{3,0,2,1:T(4,128)(2,1)} copy(bf16[4,64,4,256]{3,2,1,0:T(4,128)(2,1)S(1)} %reshape.23) | data formatting | bytes 1048576 | tf_op jit(solution)/shard_map/reshape | solution.py:695
  58.3 43.0 %sum_all.1.sums = bf16[6656,128]{1,0:T(8,128)(2,1)} custom-call(bf16[6656,128]{1,0:T(8,128)(2,1)} %get-tuple-element.14.x_ref), custom_call_target="tpu_custom_call" | custom-call | tf_op jit(solution)/shard_map/sum_all/pallas_call | solution.py:38
  101.3 3.3 %unpack.1 = (f32[64,1728]{1,0:T(8,128)}, f32[128,512]{1,0:T(8,128)}, f32[128,3456]{1,0:T(8,128)}, f32[64,1024]{1,0:T(8,128)}, f32[64,1728]{1,0:T(8,128)}) custom-call(bf16[6656,128]{1,0:T(8,128)(2,1)} %sum_all.1.sums), custom_call_target="tpu_custom_call" | custom-call | tf_op jit(solution)/shard_map/unpack/pallas_call | solution.py:38
Async XLA Ops:
  0.6 5.5 %copy-start = (bf16[64,4,4,256]{3,2,1,0:T(4,128)(2,1)S(1)}, bf16[64,4,4,256]{3,2,1,0:T(4,128)(2,1)}, u32[]{:S(2)}) copy-start(bf16[64,4,4,256]{3,2,1,0:T(4,128)(2,1)} %param.13) | copy-start | bytes 1572868
